TPU v7x, 512 devices: a whole 4x8x8 slice. The times are simulated.
512 devices in a mesh: ply: 2 (over x_lo), len: 16 (over y, core), hgt: 16 (over x_hi, z).
Axes of the slice: x: 4 (x_hi: 2, x_lo: 2; x = x_hi * 2 + x_lo), y: 8, z: 8, core: 2. Of those that a mesh axis runs over, the one named last changes fastest.
Arguments:
- plate_state: float32 [2, 10, 8, 256, 2048], P('ply', None, None, 'len', 'hgt'), may hold values from -6 to 6
- damage: int32 [2, 8, 256, 2048], P('ply', None, 'len', 'hgt'), may hold values from 0 to 4
- frame_mask: int32 [256, 2048], P('len', 'hgt'), may hold values 0 or 1
- impact_mask: int32 [256, 2048], P('len', 'hgt'), may hold values 0 or 1
Outputs:
- final_state: float32 [2, 10, 8, 256, 2048], P('ply', None, None, 'len', 'hgt')
All inputs are finite; a program needn't handle non-finite values. No bound on the sum of `frame_mask` or of `impact_mask` on one device may be relied on, other than what follows from the above.
Results may differ from a plain program's by a relative error of at most 0.0001.
Values sent between devices are 32-bit elements; how exact they have to be, the bound alone decides.
No kernel may reach another device: no remote copies, remote signals or barrier semaphores. Data moves between devices by JAX's collectives and lax.ppermute only.
A program may use at most 64 MiB of HBM per device.

v0:
```python
import jax
import jax.numpy as jnp
from jax import lax
from jax.sharding import PartitionSpec as P

STEPS = 2


time_step = 0.25
softening = 0.15
damping = 1.0
stiffness = 2.0
pressure = 2.0


def swapped(value, axis, stride):
    mask = 2**stride
    pairs = [(source, source ^ mask) for source in range(lax.axis_size(axis))]
    return lax.ppermute(value, axis, pairs)


def padded_2(cells, sides, width):
    for axis, dim in sides:
        count = lax.axis_size(axis)
        ends = count - 1
        head = lax.slice_in_dim(cells, 0, width, axis=dim)
        tail = lax.slice_in_dim(cells, cells.shape[dim] - width, cells.shape[dim], axis=dim)
        cells = jnp.concatenate(
            [
                lax.ppermute(tail, axis, [(i, (i + 1) % count) for i in range(ends)]),
                cells,
                lax.ppermute(head, axis, [((i + 1) % count, i) for i in range(ends)]),
            ],
            axis=dim,
        )
    return cells


def central(field, axis, count):

    def shifted(offset):
        return lax.slice_in_dim(field, 2 + offset, 2 + offset + count, axis=axis)

    return (8.0 * (shifted(1) - shifted(-1)) - (shifted(2) - shifted(-2))) / 12.0


def along_length(field):
    return central(field, 1, field.shape[1] - 4)[:, :, 2:-2]


def along_height(field):
    return central(field, 2, field.shape[2] - 4)[:, 2:-2, :]


def through_thickness(field):
    padded = jnp.pad(field[:, 2:-2, 2:-2], ((2, 2), (0, 0), (0, 0)))
    return central(padded, 0, field.shape[0])


def layer_weights(thick, ply_index):
    layer = jnp.arange(thick)
    bonded = jnp.where(layer == jnp.where(ply_index == 0, thick - 1, 0), 1.0, 0.0).astype(
        jnp.float32
    )
    outer = jnp.where((layer == 0) & (ply_index == 0), 1.0, 0.0).astype(jnp.float32)
    return (bonded, outer)


def surface_of(velocity, normal_disp, ply_index):
    bonded, outer = layer_weights(velocity.shape[1], ply_index)
    selected = jnp.concatenate([velocity, normal_disp[None]], axis=0)
    return jnp.sum(selected * bonded[None, :, None, None], axis=1)


def velocity_update(stress_pad, velocity, normal_disp, partner, keep_mask, push_mask, ply_index):
    bonded, outer = layer_weights(velocity.shape[1], ply_index)
    own = surface_of(velocity, normal_disp, ply_index)
    accel_x = (
        along_length(stress_pad[0]) + along_height(stress_pad[3]) + through_thickness(stress_pad[4])
    )
    accel_y = (
        along_length(stress_pad[3]) + along_height(stress_pad[1]) + through_thickness(stress_pad[5])
    )
    accel_z = (
        along_length(stress_pad[4]) + along_height(stress_pad[5]) + through_thickness(stress_pad[2])
    )
    accel_z = accel_z + pressure * push_mask[None] * outer[:, None, None]
    pull_x = damping * (partner[0] - own[0])
    pull_y = damping * (partner[1] - own[1])
    pull_z = stiffness * (partner[3] - own[3]) + damping * (partner[2] - own[2])
    traction = jnp.stack([pull_x, pull_y, pull_z])[:, None] * bonded[None, :, None, None]
    accel = jnp.stack([accel_x, accel_y, accel_z]) + traction
    return (velocity + time_step * accel) * keep_mask[None, None]


def stress_update(stress, vel_pad, levels):
    scale = 1.0 - softening * levels.astype(jnp.float32)
    grad_xx = along_length(vel_pad[0])
    grad_yy = along_height(vel_pad[1])
    grad_zz = through_thickness(vel_pad[2])
    divergence = grad_xx + grad_yy + grad_zz
    shear_xy = along_height(vel_pad[0]) + along_length(vel_pad[1])
    shear_xz = through_thickness(vel_pad[0]) + along_length(vel_pad[2])
    shear_yz = through_thickness(vel_pad[1]) + along_height(vel_pad[2])
    change = jnp.stack(
        [
            scale * divergence + 2.0 * scale * grad_xx,
            scale * divergence + 2.0 * scale * grad_yy,
            scale * divergence + 2.0 * scale * grad_zz,
            scale * shear_xy,
            scale * shear_xz,
            scale * shear_yz,
        ]
    )
    return stress + time_step * change


def finish(fields, vel_pad, levels):
    stress_new = stress_update(fields[3:9], vel_pad, levels)
    velocity = vel_pad[:, :, 2:-2, 2:-2]
    normal_disp = fields[9] + time_step * velocity[2]
    return jnp.concatenate([velocity, stress_new, normal_disp[None]], axis=0)


def per_device(plate_state, damage, frame_mask, impact_mask):
    ply_index = lax.axis_index("ply")
    fields = plate_state[0]
    levels = damage[0]
    keep_mask = (1 - frame_mask).astype(jnp.float32)
    push_mask = impact_mask.astype(jnp.float32)
    for step_index in range(STEPS):
        partner = swapped(surface_of(fields[0:3], fields[9], ply_index), "ply", 0)
        stress_pad = padded_2(fields[3:9], (("len", 2), ("hgt", 3)), 2)
        velocity = velocity_update(
            stress_pad, fields[0:3], fields[9], partner, keep_mask, push_mask, ply_index
        )
        vel_pad = padded_2(velocity, (("len", 2), ("hgt", 3)), 2)
        fields = finish(fields, vel_pad, levels)
    return fields[None]


def solution(mesh):
    placed = (
        P("ply", None, None, "len", "hgt"),
        P("ply", None, "len", "hgt"),
        P("len", "hgt"),
        P("len", "hgt"),
    )
    return jax.shard_map(
        per_device,
        mesh=mesh,
        in_specs=placed,
        out_specs=P("ply", None, None, "len", "hgt"),
        check_vma=False,
    )
```

profile of v0, /device:TPU:31, one launch (start us, length us, event | category | flops | bytes accessed | tf_op | source)
XLA Modules:
  0.0 111.3 jit_solution(6187791948104063775)
XLA Ops:
  1.2 5.0 %collective-permute-start = (f32[6,8,2,128]{3,1,2,0:T(8,128)S(1)}, f32[6,8,2,128]{3,1,2,0:T(8,128)S(1)}, u32[]{:S(2)}, u32[]{:S(2)}) collective-permute-start(f32[6,8,2,128]{3,1,2,0:T(8,128)S(1)} %get-tuple-element.39), channel_id=1, source_target_pairs={{0,16},{16,32},{32,48},{48,64},{64,80},{80,96},{96,112},{112,128},... | collective-permute-start | bytes 147464 | tf_op jit(solution)/shard_map/ppermute | solution.py:30
  6.2 1.9 %collective-permute-start.1 = (f32[6,8,2,128]{3,1,2,0:T(8,128)S(1)}, f32[6,8,2,128]{3,1,2,0:T(8,128)S(1)}, u32[]{:S(2)}, u32[]{:S(2)}) collective-permute-start(f32[6,8,2,128]{3,1,2,0:T(8,128)S(1)} %get-tuple-element.40), channel_id=1, source_target_pairs={{16,0},{32,16},{48,32},{64,48},{80,64},{96,80},{112,96},{128,112},... | collective-permute-start | bytes 147464 | tf_op jit(solution)/shard_map/ppermute | solution.py:32
  10.1 2.5 %collective-permute-start.4 = (f32[4,16,128]{2,1,0:T(8,128)S(1)}, f32[4,16,128]{2,1,0:T(8,128)S(1)}, u32[]{:S(2)}, u32[]{:S(2)}) collective-permute-start(f32[4,16,128]{2,1,0:T(8,128)S(1)} %fusion), channel_id=1, source_target_pairs={{0,256},{256,0},{1,257},{257,1},{2,258},{258,2},{3,259},{259,3},{4... | collective-permute-start | bytes 98312 | tf_op jit(solution)/shard_map/ppermute | solution.py:19
  12.6 2.4 %collective-permute-done.4 = f32[4,16,128]{2,1,0:T(8,128)S(1)} collective-permute-done((f32[4,16,128]{2,1,0:T(8,128)S(1)}, f32[4,16,128]{2,1,0:T(8,128)S(1)}, u32[]{:S(2)}, u32[]{:S(2)}) %collective-permute-start.4) | collective-permute-done | bytes 32800 | tf_op jit(solution)/shard_map/ppermute | solution.py:19
  15.6 4.0 %collective-permute-start.2 = (f32[6,8,20,2]{2,1,3,0:T(8,128)S(1)}, f32[6,8,20,2]{2,1,3,0:T(8,128)S(1)}, u32[]{:S(2)}, u32[]{:S(2)}) collective-permute-start(f32[6,8,20,2]{2,1,3,0:T(8,128)S(1)} %copy.75), channel_id=1, source_target_pairs={{0,1},{1,2},{2,3},{3,4},{4,5},{5,6},{6,7},{7,8},{8,9},{9,10},{10,1... | collective-permute-start | bytes 23048 | tf_op jit(solution)/shard_map/ppermute | solution.py:30
  20.0 9.4 %collective-permute-start.3 = (f32[6,8,20,2]{2,1,3,0:T(8,128)S(1)}, f32[6,8,20,2]{2,1,3,0:T(8,128)S(1)}, u32[]{:S(2)}, u32[]{:S(2)}) collective-permute-start(f32[6,8,20,2]{2,1,3,0:T(8,128)S(1)} %copy.76), channel_id=1, source_target_pairs={{1,0},{2,1},{3,2},{4,3},{5,4},{6,5},{7,6},{8,7},{9,8},{10,9},{11,1... | collective-permute-start | bytes 23048 | tf_op jit(solution)/shard_map/ppermute | solution.py:32
  32.8 6.6 %collective-permute-start.5 = (f32[3,8,2,128]{3,1,2,0:T(8,128)S(1)}, f32[3,8,2,128]{3,1,2,0:T(8,128)S(1)}, u32[]{:S(2)}, u32[]{:S(2)}) collective-permute-start(f32[3,8,2,128]{3,1,2,0:T(8,128)S(1)} %get-tuple-element.47), channel_id=1, source_target_pairs={{0,16},{16,32},{32,48},{48,64},{64,80},{80,96},{96,112},{112,128},... | collective-permute-start | bytes 73736 | tf_op jit(solution)/shard_map/ppermute | solution.py:30
  39.5 1.9 %collective-permute-start.6 = (f32[3,8,2,128]{3,1,2,0:T(8,128)S(1)}, f32[3,8,2,128]{3,1,2,0:T(8,128)S(1)}, u32[]{:S(2)}, u32[]{:S(2)}) collective-permute-start(f32[3,8,2,128]{3,1,2,0:T(8,128)S(1)} %get-tuple-element.48), channel_id=1, source_target_pairs={{16,0},{32,16},{48,32},{64,48},{80,64},{96,80},{112,96},{128,112},... | collective-permute-start | bytes 73736 | tf_op jit(solution)/shard_map/ppermute | solution.py:32
  41.5 4.3 %collective-permute-done.6 = f32[3,8,2,128]{3,1,2,0:T(8,128)S(1)} collective-permute-done((f32[3,8,2,128]{3,1,2,0:T(8,128)S(1)}, f32[3,8,2,128]{3,1,2,0:T(8,128)S(1)}, u32[]{:S(2)}, u32[]{:S(2)}) %collective-permute-start.6) | collective-permute-done | bytes 24608 | tf_op jit(solution)/shard_map/ppermute | solution.py:32
  46.0 1.9 %collective-permute-start.7 = (f32[3,8,20,2]{3,1,2,0:T(8,128)S(1)}, f32[3,8,20,2]{3,1,2,0:T(8,128)S(1)}, u32[]{:S(2)}, u32[]{:S(2)}) collective-permute-start(f32[3,8,20,2]{3,1,2,0:T(8,128)S(1)} %get-tuple-element.43), channel_id=1, source_target_pairs={{0,1},{1,2},{2,3},{3,4},{4,5},{5,6},{6,7},{7,8},{8,9},{9,10},{10,1... | collective-permute-start | bytes 11528 | tf_op jit(solution)/shard_map/ppermute | solution.py:30
  47.9 7.6 %collective-permute-start.8 = (f32[3,8,20,2]{3,1,2,0:T(8,128)S(1)}, f32[3,8,20,2]{3,1,2,0:T(8,128)S(1)}, u32[]{:S(2)}, u32[]{:S(2)}) collective-permute-start(f32[3,8,20,2]{3,1,2,0:T(8,128)S(1)} %get-tuple-element.44), channel_id=1, source_target_pairs={{1,0},{2,1},{3,2},{4,3},{5,4},{6,5},{7,6},{8,7},{9,8},{10,9},{11,1... | collective-permute-start | bytes 11528 | tf_op jit(solution)/shard_map/ppermute | solution.py:32
  55.6 1.9 %collective-permute-start.13 = (f32[4,16,128]{2,1,0:T(8,128)S(1)}, f32[4,16,128]{2,1,0:T(8,128)S(1)}, u32[]{:S(2)}, u32[]{:S(2)}) collective-permute-start(f32[4,16,128]{2,1,0:T(8,128)S(1)} %fusion.1), channel_id=1, source_target_pairs={{0,256},{256,0},{1,257},{257,1},{2,258},{258,2},{3,259},{259,3},{4... | collective-permute-start | bytes 98312 | tf_op jit(solution)/shard_map/ppermute | solution.py:19
  61.3 1.9 %collective-permute-start.10 = (f32[6,8,2,128]{3,1,2,0:T(8,128)S(1)}, f32[6,8,2,128]{3,1,2,0:T(8,128)S(1)}, u32[]{:S(2)}, u32[]{:S(2)}) collective-permute-start(f32[6,8,2,128]{3,1,2,0:T(8,128)S(1)} %get-tuple-element.38), channel_id=1, source_target_pairs={{16,0},{32,16},{48,32},{64,48},{80,64},{96,80},{112,96},{128,112},... | collective-permute-start | bytes 147464 | tf_op jit(solution)/shard_map/ppermute | solution.py:32
  63.2 4.9 %collective-permute-start.9 = (f32[6,8,2,128]{3,1,2,0:T(8,128)S(1)}, f32[6,8,2,128]{3,1,2,0:T(8,128)S(1)}, u32[]{:S(2)}, u32[]{:S(2)}) collective-permute-start(f32[6,8,2,128]{3,1,2,0:T(8,128)S(1)} %get-tuple-element.37), channel_id=1, source_target_pairs={{0,16},{16,32},{32,48},{48,64},{64,80},{80,96},{96,112},{112,128},... | collective-permute-start | bytes 147464 | tf_op jit(solution)/shard_map/ppermute | solution.py:30
  68.1 1.1 %collective-permute-done.9 = f32[6,8,2,128]{3,1,2,0:T(8,128)S(1)} collective-permute-done((f32[6,8,2,128]{3,1,2,0:T(8,128)S(1)}, f32[6,8,2,128]{3,1,2,0:T(8,128)S(1)}, u32[]{:S(2)}, u32[]{:S(2)}) %collective-permute-start.9) | collective-permute-done | bytes 49184 | tf_op jit(solution)/shard_map/ppermute | solution.py:30
  69.8 1.9 %collective-permute-start.11 = (f32[6,8,20,2]{2,1,3,0:T(8,128)S(1)}, f32[6,8,20,2]{2,1,3,0:T(8,128)S(1)}, u32[]{:S(2)}, u32[]{:S(2)}) collective-permute-start(f32[6,8,20,2]{2,1,3,0:T(8,128)S(1)} %copy.78), channel_id=1, source_target_pairs={{0,1},{1,2},{2,3},{3,4},{4,5},{5,6},{6,7},{7,8},{8,9},{9,10},{10,1... | collective-permute-start | bytes 23048 | tf_op jit(solution)/shard_map/ppermute | solution.py:30
  72.1 7.5 %collective-permute-start.12 = (f32[6,8,20,2]{2,1,3,0:T(8,128)S(1)}, f32[6,8,20,2]{2,1,3,0:T(8,128)S(1)}, u32[]{:S(2)}, u32[]{:S(2)}) collective-permute-start(f32[6,8,20,2]{2,1,3,0:T(8,128)S(1)} %copy.79), channel_id=1, source_target_pairs={{1,0},{2,1},{3,2},{4,3},{5,4},{6,5},{7,6},{8,7},{9,8},{10,9},{11,1... | collective-permute-start | bytes 23048 | tf_op jit(solution)/shard_map/ppermute | solution.py:32
  83.1 6.3 %collective-permute-start.14 = (f32[3,8,2,128]{3,1,2,0:T(8,128)S(1)}, f32[3,8,2,128]{3,1,2,0:T(8,128)S(1)}, u32[]{:S(2)}, u32[]{:S(2)}) collective-permute-start(f32[3,8,2,128]{3,1,2,0:T(8,128)S(1)} %get-tuple-element.45), channel_id=1, source_target_pairs={{0,16},{16,32},{32,48},{48,64},{64,80},{80,96},{96,112},{112,128},... | collective-permute-start | bytes 73736 | tf_op jit(solution)/shard_map/ppermute | solution.py:30
  89.5 1.9 %collective-permute-start.15 = (f32[3,8,2,128]{3,1,2,0:T(8,128)S(1)}, f32[3,8,2,128]{3,1,2,0:T(8,128)S(1)}, u32[]{:S(2)}, u32[]{:S(2)}) collective-permute-start(f32[3,8,2,128]{3,1,2,0:T(8,128)S(1)} %get-tuple-element.46), channel_id=1, source_target_pairs={{16,0},{32,16},{48,32},{64,48},{80,64},{96,80},{112,96},{128,112},... | collective-permute-start | bytes 73736 | tf_op jit(solution)/shard_map/ppermute | solution.py:32
  91.4 4.4 %collective-permute-done.15 = f32[3,8,2,128]{3,1,2,0:T(8,128)S(1)} collective-permute-done((f32[3,8,2,128]{3,1,2,0:T(8,128)S(1)}, f32[3,8,2,128]{3,1,2,0:T(8,128)S(1)}, u32[]{:S(2)}, u32[]{:S(2)}) %collective-permute-start.15) | collective-permute-done | bytes 24608 | tf_op jit(solution)/shard_map/ppermute | solution.py:32
  96.0 1.9 %collective-permute-start.16 = (f32[3,8,20,2]{3,1,2,0:T(8,128)S(1)}, f32[3,8,20,2]{3,1,2,0:T(8,128)S(1)}, u32[]{:S(2)}, u32[]{:S(2)}) collective-permute-start(f32[3,8,20,2]{3,1,2,0:T(8,128)S(1)} %get-tuple-element.41), channel_id=1, source_target_pairs={{0,1},{1,2},{2,3},{3,4},{4,5},{5,6},{6,7},{7,8},{8,9},{9,10},{10,1... | collective-permute-start | bytes 11528 | tf_op jit(solution)/shard_map/ppermute | solution.py:30
  97.9 7.6 %collective-permute-start.17 = (f32[3,8,20,2]{3,1,2,0:T(8,128)S(1)}, f32[3,8,20,2]{3,1,2,0:T(8,128)S(1)}, u32[]{:S(2)}, u32[]{:S(2)}) collective-permute-start(f32[3,8,20,2]{3,1,2,0:T(8,128)S(1)} %get-tuple-element.42), channel_id=1, source_target_pairs={{1,0},{2,1},{3,2},{4,3},{5,4},{6,5},{7,6},{8,7},{9,8},{10,9},{11,1... | collective-permute-start | bytes 11528 | tf_op jit(solution)/shard_map/ppermute | solution.py:32
  105.6 1.6 %collective-permute-done.16 = f32[3,8,20,2]{3,1,2,0:T(8,128)S(1)} collective-permute-done((f32[3,8,20,2]{3,1,2,0:T(8,128)S(1)}, f32[3,8,20,2]{3,1,2,0:T(8,128)S(1)}, u32[]{:S(2)}, u32[]{:S(2)}) %collective-permute-start.16) | collective-permute-done | bytes 3872 | tf_op jit(solution)/shard_map/ppermute | solution.py:30
  107.1 1.5 %collective-permute-done.17 = f32[3,8,20,2]{3,1,2,0:T(8,128)S(1)} collective-permute-done((f32[3,8,20,2]{3,1,2,0:T(8,128)S(1)}, f32[3,8,20,2]{3,1,2,0:T(8,128)S(1)}, u32[]{:S(2)}, u32[]{:S(2)}) %collective-permute-start.17) | collective-permute-done | bytes 3872 | tf_op jit(solution)/shard_map/ppermute | solution.py:32
  (126 shorter events, 18.7 us)
Async XLA Ops:
  1.2 13.8 %collective-permute-start = (f32[6,8,2,128]{3,1,2,0:T(8,128)S(1)}, f32[6,8,2,128]{3,1,2,0:T(8,128)S(1)}, u32[]{:S(2)}, u32[]{:S(2)}) collective-permute-start(f32[6,8,2,128]{3,1,2,0:T(8,128)S(1)} %get-tuple-element.39), channel_id=1, source_target_pairs={{0,16},{16,32},{32,48},{48,64},{64,80},{80,96},{96,112},{112,128},... | collective-permute-start | bytes 147464 | tf_op jit(solution)/shard_map/ppermute | solution.py:30
  6.2 8.8 %collective-permute-start.1 = (f32[6,8,2,128]{3,1,2,0:T(8,128)S(1)}, f32[6,8,2,128]{3,1,2,0:T(8,128)S(1)}, u32[]{:S(2)}, u32[]{:S(2)}) collective-permute-start(f32[6,8,2,128]{3,1,2,0:T(8,128)S(1)} %get-tuple-element.40), channel_id=1, source_target_pairs={{16,0},{32,16},{48,32},{64,48},{80,64},{96,80},{112,96},{128,112},... | collective-permute-start | bytes 147464 | tf_op jit(solution)/shard_map/ppermute | solution.py:32
  10.0 2.6 %copy-start.1 = (s32[16,128]{1,0:T(8,128)S(1)}, s32[16,128]{1,0:T(8,128)}, u32[]{:S(2)}) copy-start(s32[16,128]{1,0:T(8,128)} %param.7) | copy-start | bytes 24580
  10.1 2.5 %copy-start.2 = (s32[16,128]{1,0:T(8,128)S(1)}, s32[16,128]{1,0:T(8,128)}, u32[]{:S(2)}) copy-start(s32[16,128]{1,0:T(8,128)} %param.6) | copy-start | bytes 24580
  10.1 4.9 %collective-permute-start.4 = (f32[4,16,128]{2,1,0:T(8,128)S(1)}, f32[4,16,128]{2,1,0:T(8,128)S(1)}, u32[]{:S(2)}, u32[]{:S(2)}) collective-permute-start(f32[4,16,128]{2,1,0:T(8,128)S(1)} %fusion), channel_id=1, source_target_pairs={{0,256},{256,0},{1,257},{257,1},{2,258},{258,2},{3,259},{259,3},{4... | collective-permute-start | bytes 98312 | tf_op jit(solution)/shard_map/ppermute | solution.py:19
  15.6 13.8 %collective-permute-start.2 = (f32[6,8,20,2]{2,1,3,0:T(8,128)S(1)}, f32[6,8,20,2]{2,1,3,0:T(8,128)S(1)}, u32[]{:S(2)}, u32[]{:S(2)}) collective-permute-start(f32[6,8,20,2]{2,1,3,0:T(8,128)S(1)} %copy.75), channel_id=1, source_target_pairs={{0,1},{1,2},{2,3},{3,4},{4,5},{5,6},{6,7},{7,8},{8,9},{9,10},{10,1... | collective-permute-start | bytes 23048 | tf_op jit(solution)/shard_map/ppermute | solution.py:30
  20.0 10.6 %collective-permute-start.3 = (f32[6,8,20,2]{2,1,3,0:T(8,128)S(1)}, f32[6,8,20,2]{2,1,3,0:T(8,128)S(1)}, u32[]{:S(2)}, u32[]{:S(2)}) collective-permute-start(f32[6,8,20,2]{2,1,3,0:T(8,128)S(1)} %copy.76), channel_id=1, source_target_pairs={{1,0},{2,1},{3,2},{4,3},{5,4},{6,5},{7,6},{8,7},{9,8},{10,9},{11,1... | collective-permute-start | bytes 23048 | tf_op jit(solution)/shard_map/ppermute | solution.py:32
  32.8 8.7 %collective-permute-start.5 = (f32[3,8,2,128]{3,1,2,0:T(8,128)S(1)}, f32[3,8,2,128]{3,1,2,0:T(8,128)S(1)}, u32[]{:S(2)}, u32[]{:S(2)}) collective-permute-start(f32[3,8,2,128]{3,1,2,0:T(8,128)S(1)} %get-tuple-element.47), channel_id=1, source_target_pairs={{0,16},{16,32},{32,48},{48,64},{64,80},{80,96},{96,112},{112,128},... | collective-permute-start | bytes 73736 | tf_op jit(solution)/shard_map/ppermute | solution.py:30
  39.5 6.4 %collective-permute-start.6 = (f32[3,8,2,128]{3,1,2,0:T(8,128)S(1)}, f32[3,8,2,128]{3,1,2,0:T(8,128)S(1)}, u32[]{:S(2)}, u32[]{:S(2)}) collective-permute-start(f32[3,8,2,128]{3,1,2,0:T(8,128)S(1)} %get-tuple-element.48), channel_id=1, source_target_pairs={{16,0},{32,16},{48,32},{64,48},{80,64},{96,80},{112,96},{128,112},... | collective-permute-start | bytes 73736 | tf_op jit(solution)/shard_map/ppermute | solution.py:32
  46.0 11.5 %collective-permute-start.7 = (f32[3,8,20,2]{3,1,2,0:T(8,128)S(1)}, f32[3,8,20,2]{3,1,2,0:T(8,128)S(1)}, u32[]{:S(2)}, u32[]{:S(2)}) collective-permute-start(f32[3,8,20,2]{3,1,2,0:T(8,128)S(1)} %get-tuple-element.43), channel_id=1, source_target_pairs={{0,1},{1,2},{2,3},{3,4},{4,5},{5,6},{6,7},{7,8},{8,9},{9,10},{10,1... | collective-permute-start | bytes 11528 | tf_op jit(solution)/shard_map/ppermute | solution.py:30
  47.9 10.7 %collective-permute-start.8 = (f32[3,8,20,2]{3,1,2,0:T(8,128)S(1)}, f32[3,8,20,2]{3,1,2,0:T(8,128)S(1)}, u32[]{:S(2)}, u32[]{:S(2)}) collective-permute-start(f32[3,8,20,2]{3,1,2,0:T(8,128)S(1)} %get-tuple-element.44), channel_id=1, source_target_pairs={{1,0},{2,1},{3,2},{4,3},{5,4},{6,5},{7,6},{8,7},{9,8},{10,9},{11,1... | collective-permute-start | bytes 11528 | tf_op jit(solution)/shard_map/ppermute | solution.py:32
  55.6 12.5 %collective-permute-start.13 = (f32[4,16,128]{2,1,0:T(8,128)S(1)}, f32[4,16,128]{2,1,0:T(8,128)S(1)}, u32[]{:S(2)}, u32[]{:S(2)}) collective-permute-start(f32[4,16,128]{2,1,0:T(8,128)S(1)} %fusion.1), channel_id=1, source_target_pairs={{0,256},{256,0},{1,257},{257,1},{2,258},{258,2},{3,259},{259,3},{4... | collective-permute-start | bytes 98312 | tf_op jit(solution)/shard_map/ppermute | solution.py:19
  59.6 0.8 copy-start
  61.3 6.8 %collective-permute-start.10 = (f32[6,8,2,128]{3,1,2,0:T(8,128)S(1)}, f32[6,8,2,128]{3,1,2,0:T(8,128)S(1)}, u32[]{:S(2)}, u32[]{:S(2)}) collective-permute-start(f32[6,8,2,128]{3,1,2,0:T(8,128)S(1)} %get-tuple-element.38), channel_id=1, source_target_pairs={{16,0},{32,16},{48,32},{64,48},{80,64},{96,80},{112,96},{128,112},... | collective-permute-start | bytes 147464 | tf_op jit(solution)/shard_map/ppermute | solution.py:32
  63.2 6.0 %collective-permute-start.9 = (f32[6,8,2,128]{3,1,2,0:T(8,128)S(1)}, f32[6,8,2,128]{3,1,2,0:T(8,128)S(1)}, u32[]{:S(2)}, u32[]{:S(2)}) collective-permute-start(f32[6,8,2,128]{3,1,2,0:T(8,128)S(1)} %get-tuple-element.37), channel_id=1, source_target_pairs={{0,16},{16,32},{32,48},{48,64},{64,80},{80,96},{96,112},{112,128},... | collective-permute-start | bytes 147464 | tf_op jit(solution)/shard_map/ppermute | solution.py:30
  69.8 9.8 %collective-permute-start.11 = (f32[6,8,20,2]{2,1,3,0:T(8,128)S(1)}, f32[6,8,20,2]{2,1,3,0:T(8,128)S(1)}, u32[]{:S(2)}, u32[]{:S(2)}) collective-permute-start(f32[6,8,20,2]{2,1,3,0:T(8,128)S(1)} %copy.78), channel_id=1, source_target_pairs={{0,1},{1,2},{2,3},{3,4},{4,5},{5,6},{6,7},{7,8},{8,9},{9,10},{10,1... | collective-permute-start | bytes 23048 | tf_op jit(solution)/shard_map/ppermute | solution.py:30
  72.1 8.6 %collective-permute-start.12 = (f32[6,8,20,2]{2,1,3,0:T(8,128)S(1)}, f32[6,8,20,2]{2,1,3,0:T(8,128)S(1)}, u32[]{:S(2)}, u32[]{:S(2)}) collective-permute-start(f32[6,8,20,2]{2,1,3,0:T(8,128)S(1)} %copy.79), channel_id=1, source_target_pairs={{1,0},{2,1},{3,2},{4,3},{5,4},{6,5},{7,6},{8,7},{9,8},{10,9},{11,1... | collective-permute-start | bytes 23048 | tf_op jit(solution)/shard_map/ppermute | solution.py:32
  83.1 8.2 %collective-permute-start.14 = (f32[3,8,2,128]{3,1,2,0:T(8,128)S(1)}, f32[3,8,2,128]{3,1,2,0:T(8,128)S(1)}, u32[]{:S(2)}, u32[]{:S(2)}) collective-permute-start(f32[3,8,2,128]{3,1,2,0:T(8,128)S(1)} %get-tuple-element.45), channel_id=1, source_target_pairs={{0,16},{16,32},{32,48},{48,64},{64,80},{80,96},{96,112},{112,128},... | collective-permute-start | bytes 73736 | tf_op jit(solution)/shard_map/ppermute | solution.py:30
  89.5 6.4 %collective-permute-start.15 = (f32[3,8,2,128]{3,1,2,0:T(8,128)S(1)}, f32[3,8,2,128]{3,1,2,0:T(8,128)S(1)}, u32[]{:S(2)}, u32[]{:S(2)}) collective-permute-start(f32[3,8,2,128]{3,1,2,0:T(8,128)S(1)} %get-tuple-element.46), channel_id=1, source_target_pairs={{16,0},{32,16},{48,32},{64,48},{80,64},{96,80},{112,96},{128,112},... | collective-permute-start | bytes 73736 | tf_op jit(solution)/shard_map/ppermute | solution.py:32
  96.0 11.2 %collective-permute-start.16 = (f32[3,8,20,2]{3,1,2,0:T(8,128)S(1)}, f32[3,8,20,2]{3,1,2,0:T(8,128)S(1)}, u32[]{:S(2)}, u32[]{:S(2)}) collective-permute-start(f32[3,8,20,2]{3,1,2,0:T(8,128)S(1)} %get-tuple-element.41), channel_id=1, source_target_pairs={{0,1},{1,2},{2,3},{3,4},{4,5},{5,6},{6,7},{7,8},{8,9},{9,10},{10,1... | collective-permute-start | bytes 11528 | tf_op jit(solution)/shard_map/ppermute | solution.py:30
  97.9 10.7 %collective-permute-start.17 = (f32[3,8,20,2]{3,1,2,0:T(8,128)S(1)}, f32[3,8,20,2]{3,1,2,0:T(8,128)S(1)}, u32[]{:S(2)}, u32[]{:S(2)}) collective-permute-start(f32[3,8,20,2]{3,1,2,0:T(8,128)S(1)} %get-tuple-element.42), channel_id=1, source_target_pairs={{1,0},{2,1},{3,2},{4,3},{5,4},{6,5},{7,6},{8,7},{9,8},{10,9},{11,1... | collective-permute-start | bytes 11528 | tf_op jit(solution)/shard_map/ppermute | solution.py:32
where the time goes:
time: 112 us; the launch traced here: 111 us
  starting transfers between devices  76.6 us (68%)
  waiting for transfers between devices  17.8 us (16%)
  local copies, waits for them, and re-layouts  10.9 us (10%)
  other arithmetic  5.26 us (5%)
    ppermute x8, starting transfers between devices, padded_2(): lax.ppermute(head, axis, [((i + 1) % count, i) for i in range(ends)])  39.7 us
    ppermute x8, starting transfers between devices, padded_2(): lax.ppermute(tail, axis, [(i, (i + 1) % count) for i in range(ends)])  32.5 us
    ppermute x8, waiting for transfers between devices, padded_2(): lax.ppermute(head, axis, [((i + 1) % count, i) for i in range(ends)])  12.7 us
    ppermute x2, starting transfers between devices, swapped(): return lax.ppermute(value, axis, pairs)  4.38 us
    ppermute x8, waiting for transfers between devices, padded_2(): lax.ppermute(tail, axis, [(i, (i + 1) % count) for i in range(ends)])  2.69 us
    unnamed x12, local copies, waits for them, and re-layouts  2.49 us
    ppermute x2, waiting for transfers between devices, swapped(): return lax.ppermute(value, axis, pairs)  2.38 us
  transfers between devices with their start and end apart: 18, of which 9 were waited for; matrix products, arithmetic and copies ran while one was open for 5% of the time, Pallas kernels for 0%

commit v1 on v0

v1 whole, which is shorter than its diff:
```python
import functools

import jax
import jax.numpy as jnp
from jax import lax
from jax.experimental import pallas as pl
from jax.experimental.pallas import tpu as pltpu
from jax.sharding import PartitionSpec as P

time_step = 0.25
softening = 0.15
damping = 1.0
stiffness = 2.0
pressure = 2.0

THICK = 8
ROWS = 16
LANES = 128
HALO = 8
EXT = ROWS + 2 * HALO

SCALE = 72
DISP = 80
MATE = 81
KEEP = 96
PUSH = 97
PLANES = 98
PER_GROUP = 16
GROUPS = 7

STORE = 48
TOP = 16

STRIDE = THICK + 2
VX, VY, VZ, SXX, SYY, SZZ, SXY, SXZ, SYZ = range(9)
FIELD_PLANES = 9 * STRIDE + 2

VMEM = pl.BlockSpec(memory_space=pltpu.VMEM)
PAIRS_EVEN = [[2 * i, 2 * i + 1] for i in range(8)]


def pair_groups(count, first):
    return [[(i + first) % count, (i + first + 1) % count] for i in range(0, count, 2)]


def surface_kernel(state, out):
    front = lax.axis_index("ply") == 0

    def layer(field, depth):
        return jnp.where(front, state[0, field, THICK - 1 - depth], state[0, field, depth])

    picks = [(f, 0) for f in (0, 1, 2, 9, 3, 4, 6, 7, 8)]
    picks += [(f, depth) for depth in (1, 2) for f in (7, 8, 5)]
    for k, (field, depth) in enumerate(picks):
        out[k] = layer(field, depth)


def write_tile(state, damage, frame, impact, mate, out, rows, size, front):
    for field in range(9):
        for z in range(THICK):
            out(field * THICK + z, state[0, field, z, rows, :])
    for z in range(THICK):
        out(SCALE + z, 1.0 - softening * damage[0, z, rows, :].astype(jnp.float32))
    out(DISP, jnp.where(front, state[0, 9, THICK - 1, rows, :], state[0, 9, 0, rows, :]))
    for k in range(15):
        out(MATE + k, jnp.where(front, mate[1, k, rows, :], mate[0, k, rows, :]))
    out(KEEP, (1 - frame[rows, :]).astype(jnp.float32))
    out(PUSH, impact[rows, :].astype(jnp.float32))


def length_kernel(state, damage, frame, impact, mate, near, far):
    front = lax.axis_index("ply") == 0
    core = lax.axis_index("len") % 2
    for out, start in ((near, (1 - core) * HALO), (far, core * HALO)):
        rows = pl.ds(pl.multiple_of(start, HALO), HALO)

        def put(plane, value, out=out):
            out[plane] = value

        write_tile(state, damage, frame, impact, mate, put, rows, HALO, front)


def height_kernel(state, damage, frame, impact, mate, near, far, ext, right, left):
    front = lax.axis_index("ply") == 0
    index = lax.axis_index("len")
    core = index % 2
    has_top = index > 0
    has_bottom = index < lax.axis_size("len") - 1

    def put(plane, value):
        ext[plane, HALO : HALO + ROWS, :] = value

    write_tile(state, damage, frame, impact, mate, put, slice(0, ROWS), ROWS, front)
    for plane in range(PLANES):
        top = jnp.where(core == 0, far[0, plane], near[0, plane])
        bottom = jnp.where(core == 0, near[1, plane], far[1, plane])
        ext[plane, 0:HALO, :] = jnp.where(has_top, top, 0.0)
        ext[plane, HALO + ROWS : EXT, :] = jnp.where(has_bottom, bottom, 0.0)
    slot = lax.broadcasted_iota(jnp.int32, (EXT, LANES), 1) // HALO
    for g in range(GROUPS):
        first = jnp.zeros((EXT, LANES), jnp.float32)
        last = first
        for j in range(min(PER_GROUP, PLANES - g * PER_GROUP)):
            plane = ext[g * PER_GROUP + j]
            head = pltpu.roll(plane, HALO * j, 1) if j else plane
            tail = pltpu.roll(plane, (HALO * j + HALO) % LANES, 1) if j < 15 else plane
            first = jnp.where(slot == j, head, first)
            last = jnp.where(slot == j, tail, last)
        left[g] = first
        right[g] = last


def lane_shift(x, s):
    lane = lax.broadcasted_iota(jnp.int32, x.shape, 2)
    turned = pltpu.roll(x, (-s) % LANES, 2)
    other = jnp.concatenate([turned[1:2], turned[0:1]], axis=0)
    inside = lane < LANES - s if s > 0 else lane >= -s
    return jnp.where(inside, turned, other)


def along_height(x):
    a = x - lane_shift(x, -2)
    b = 8.0 * a - lane_shift(a, 1)
    return lane_shift(b, 1) - a


def main_kernel(state, ext, near, far, out, fields, scale, extra):
    front = lax.axis_index("ply") == 0
    place = lax.axis_index("hgt")
    odd = place % 2
    has_left = place > 0
    has_right = place < lax.axis_size("hgt") - 1
    bonded = jnp.where(front, THICK - 1, 0)
    rows_all = slice(TOP - HALO, TOP + ROWS + HALO)

    zero = jnp.zeros((2, STORE, LANES), jnp.float32)
    for f in range(10):
        fields[f * STRIDE] = zero
        fields[f * STRIDE + 1] = zero

    lane = lax.broadcasted_iota(jnp.int32, (EXT, LANES), 1)
    is_right = (lane < HALO) & has_right
    is_left = (lane >= LANES - HALO) & has_left
    for g in range(GROUPS):
        from_right = jnp.where(odd == 0, near[1, g], far[1, g])
        from_left = jnp.where(odd == 0, far[0, g], near[0, g])
        for j in range(min(PER_GROUP, PLANES - g * PER_GROUP)):
            plane = g * PER_GROUP + j
            r = pltpu.roll(from_right, LANES - HALO * j, 1) if j else from_right
            m = pltpu.roll(from_left, LANES - HALO - HALO * j, 1) if j < 15 else from_left
            side = jnp.where(is_right, r, jnp.where(is_left, m, 0.0))
            if plane < SCALE:
                ref, at = fields, plane // THICK * STRIDE + 2 + plane % THICK
            elif plane < DISP:
                ref, at = scale, plane - SCALE
            else:
                ref, at = extra, plane - DISP
            ref[at, 0, rows_all, :] = ext[plane]
            ref[at, 1, rows_all, :] = side

    mate_at, keep_at, push_at = MATE - DISP, KEEP - DISP, PUSH - DISP
    step = time_step / 12.0

    def along_length(ref, at, r0, n):
        def tap(d):
            return ref[at, :, r0 + d : r0 + d + n, :]

        return 8.0 * (tap(1) - tap(-1)) - (tap(2) - tap(-2))

    def through(f, z, r0, n):
        def tap(d):
            return fields[f * STRIDE + 2 + z + d, :, r0 : r0 + n, :]

        return 8.0 * (tap(1) - tap(-1)) - (tap(2) - tap(-2))

    def spot(f, z):
        return f * STRIDE + 2 + z

    def velocities(r0, n, with_mate):
        keep = extra[keep_at, :, r0 : r0 + n, :]
        own = [fields[spot(f, bonded), :, r0 : r0 + n, :] for f in (VX, VY, VZ)]
        own.append(extra[0, :, r0 : r0 + n, :])
        mate = [extra[mate_at + k, :, r0 : r0 + n, :] for k in range(4)]
        pull = [
            damping * (mate[0] - own[0]),
            damping * (mate[1] - own[1]),
            stiffness * (mate[3] - own[3]) + damping * (mate[2] - own[2]),
        ]

        def body(z, carry):
            for v, a, b, c in ((VX, SXX, SXY, SXZ), (VY, SXY, SYY, SYZ), (VZ, SXZ, SYZ, SZZ)):
                total = (
                    along_length(fields, spot(a, z), r0, n)
                    + along_height(fields[spot(b, z), :, r0 : r0 + n, :])
                    + through(c, z, r0, n)
                )
                old = fields[spot(v, z), :, r0 : r0 + n, :]
                fields[spot(v, z), :, r0 : r0 + n, :] = (old + step * total) * keep
            return carry

        lax.fori_loop(0, THICK, body, 0)
        for f in range(3):
            at = spot(f, bonded)
            fields[at, :, r0 : r0 + n, :] += time_step * pull[f] * keep
        push = extra[push_at, :, r0 : r0 + n, :] * keep
        at = spot(VZ, 0)
        fields[at, :, r0 : r0 + n, :] += jnp.where(front, time_step * pressure, 0.0) * push

        if with_mate:
            sign = jnp.where(front, 1.0, -1.0)
            inner = lambda k: extra[mate_at + k, :, r0 : r0 + n, :]
            fresh = []
            for f, (a, b, one, two) in enumerate(((4, 6, 9, 12), (6, 5, 10, 13), (7, 8, 11, 14))):
                total = (
                    along_length(extra, mate_at + a, r0, n)
                    + along_height(extra[mate_at + b, :, r0 : r0 + n, :])
                    + sign * (8.0 * inner(one) - inner(two))
                )
                fresh.append((mate[f] + step * total - time_step * pull[f]) * keep)
            for f in range(3):
                extra[mate_at + f, :, r0 : r0 + n, :] = fresh[f]
            extra[mate_at + 3, :, r0 : r0 + n, :] = mate[3] + time_step * fresh[2]
            extra[0, :, r0 : r0 + n, :] = (
                own[3] + time_step * fields[spot(VZ, bonded), :, r0 : r0 + n, :]
            )

    def changes(z, r0, n, size):
        def cut(x):
            return x[:size]

        def length_of(f):
            return cut(along_length(fields, spot(f, z), r0, n))

        def height_of(f):
            return cut(along_height(fields[spot(f, z), :, r0 : r0 + n, :]))

        def depth_of(f):
            return cut(through(f, z, r0, n))

        factor = step * scale[z, 0:size, r0 : r0 + n, :]
        xx, yy, zz = length_of(VX), height_of(VY), depth_of(VZ)
        whole = xx + yy + zz
        return (
            factor * (whole + 2.0 * xx),
            factor * (whole + 2.0 * yy),
            factor * (whole + 2.0 * zz),
            factor * (height_of(VX) + length_of(VY)),
            factor * (depth_of(VX) + length_of(VZ)),
            factor * (depth_of(VY) + height_of(VZ)),
        )

    velocities(TOP - HALO, EXT, True)

    def first_stress(z, carry):
        r0, n = TOP - 4, ROWS + 8
        for f, change in enumerate(changes(z, r0, n, 2)):
            fields[spot(SXX + f, z), :, r0 : r0 + n, :] += change
        out[0, 9, z] = state[0, 9, z] + time_step * fields[spot(VZ, z), 0, TOP : TOP + ROWS, :]
        return carry

    lax.fori_loop(0, THICK, first_stress, 0)
    velocities(TOP - 4, ROWS + 8, False)

    def last_stress(z, carry):
        for f in range(3):
            out[0, f, z] = fields[spot(f, z), 0, TOP : TOP + ROWS, :]
        for f, change in enumerate(changes(z, TOP, ROWS, 1)):
            out[0, 3 + f, z] = fields[spot(SXX + f, z), 0, TOP : TOP + ROWS, :] + change[0]
        out[0, 9, z] += time_step * fields[spot(VZ, z), 0, TOP : TOP + ROWS, :]
        return carry

    lax.fori_loop(0, THICK, last_stress, 0)


def shaped(*shape):
    return jax.ShapeDtypeStruct(shape, jnp.float32)


def call(kernel, outs, args, **more):
    return pl.pallas_call(
        kernel,
        out_shape=outs,
        in_specs=[VMEM] * len(args),
        out_specs=jax.tree.map(lambda _: VMEM, outs),
        compiler_params=pltpu.CompilerParams(vmem_limit_bytes=32 * 2**20),
        **more,
    )(*args)


def per_device(plate_state, damage, frame_mask, impact_mask):
    even, odd = pair_groups(16, 0), pair_groups(16, 1)
    surface = call(surface_kernel, shaped(15, ROWS, LANES), (plate_state,))
    mate = lax.all_gather(surface, "ply")
    local = (plate_state, damage, frame_mask, impact_mask, mate)
    near, far = call(length_kernel, [shaped(PLANES, HALO, LANES)] * 2, local)
    near = lax.all_gather(near, "len", axis_index_groups=even)
    far = lax.all_gather(far, "len", axis_index_groups=odd)
    ext, right, left = call(
        height_kernel,
        [shaped(PLANES, EXT, LANES), shaped(GROUPS, EXT, LANES), shaped(GROUPS, EXT, LANES)],
        local + (near, far),
    )
    even_place = lax.axis_index("hgt") % 2 == 0
    near = lax.all_gather(jnp.where(even_place, right, left), "hgt", axis_index_groups=even)
    far = lax.all_gather(jnp.where(even_place, left, right), "hgt", axis_index_groups=odd)
    return call(
        main_kernel,
        shaped(1, 10, THICK, ROWS, LANES),
        (plate_state, ext, near, far),
        scratch_shapes=[
            pltpu.VMEM((FIELD_PLANES, 2, STORE, LANES), jnp.float32),
            pltpu.VMEM((THICK, 2, STORE, LANES), jnp.float32),
            pltpu.VMEM((PLANES - DISP, 2, STORE, LANES), jnp.float32),
        ],
    )


def solution(mesh):
    placed = (
        P("ply", None, None, "len", "hgt"),
        P("ply", None, "len", "hgt"),
        P("len", "hgt"),
        P("len", "hgt"),
    )
    return jax.shard_map(
        per_device,
        mesh=mesh,
        in_specs=placed,
        out_specs=P("ply", None, None, "len", "hgt"),
        check_vma=False,
    )
```

time: 112 us -> 52.4 us (0.47)
  the two profiles are of different devices: /device:TPU:31 before, /device:TPU:56 now
where the time goes in v1:
time: 52.4 us; the launch traced here: 52.1 us
  blocking collectives  38 us (73%)
  Pallas kernels  10.6 us (20%)
  local copies, waits for them, and re-layouts  3.33 us (6%)
    all_gather x1, blocking collectives, per_device(): lax.all_gather(jnp.where(even_place, left, right), 'hgt', axis_index_grou...  15.7 us
    pallas_call x4, Pallas kernels, call(): pl.pallas_call(kernel, out_shape=outs, in_specs=[VMEM] * len(args), out_s...  10.6 us
    all_gather x1, blocking collectives, per_device(): far = lax.all_gather(far, 'len', axis_index_groups=odd)  7.95 us
    all_gather x1, blocking collectives, per_device(): lax.all_gather(jnp.where(even_place, right, left), 'hgt', axis_index_grou...  6.3 us
    all_gather x1, blocking collectives, per_device(): mate = lax.all_gather(surface, 'ply')  5.74 us
    unnamed x12, local copies, waits for them, and re-layouts  3.33 us
    all_gather x1, blocking collectives, per_device(): near = lax.all_gather(near, 'len', axis_index_groups=even)  2.38 us

profile of v1, /device:TPU:56, one launch (start us, length us, event | category | flops | bytes accessed | tf_op | source)
XLA Modules:
  0.0 52.1 jit_solution(6515144389180264816)
XLA Ops:
  0.0 0.0 copy-start
  0.0 1.1 %copy-done = f32[1,10,8,16,128]{4,3,2,1,0:T(8,128)S(1)} copy-done((f32[1,10,8,16,128]{4,3,2,1,0:T(8,128)S(1)}, f32[1,10,8,16,128]{4,3,2,1,0:T(8,128)}, u32[]{:S(2)}) %copy-start) | copy-done | bytes 655384
  1.1 5.7 %all-gather = f32[30,16,128]{2,1,0:T(8,128)S(1)} all-gather(f32[15,16,128]{2,1,0:T(8,128)S(1)} %shard_map.46), channel_id=2, replica_groups=mesh['ply'=2,'len'=16,'hgt'=16] {'ply'}, dimensions={0}, use_global_device_ids=true | all-gather | bytes 368640 | tf_op jit(solution)/shard_map/all_gather | solution.py:293
  6.9 0.0 copy-start.2
  6.9 0.8 %copy-done.2 = s32[1,8,16,128]{3,2,1,0:T(8,128)S(1)} copy-done((s32[1,8,16,128]{3,2,1,0:T(8,128)S(1)}, s32[1,8,16,128]{3,2,1,0:T(8,128)}, u32[]{:S(2)}) %copy-start.2) | copy-done | bytes 65560
  7.7 0.0 copy-start.3
  7.7 0.7 %copy-done.3 = s32[16,128]{1,0:T(8,128)S(1)} copy-done((s32[16,128]{1,0:T(8,128)S(1)}, s32[16,128]{1,0:T(8,128)}, u32[]{:S(2)}) %copy-start.3) | copy-done | bytes 8216
  8.4 0.0 copy-start.4
  8.4 0.7 %copy-done.4 = s32[16,128]{1,0:T(8,128)S(1)} copy-done((s32[16,128]{1,0:T(8,128)S(1)}, s32[16,128]{1,0:T(8,128)}, u32[]{:S(2)}) %copy-start.4) | copy-done | bytes 8216
  9.1 0.0 copy-start.5
  9.1 0.1 shard_map.47
  9.2 2.4 %all-gather.1 = f32[196,8,128]{2,1,0:T(8,128)S(1)} all-gather(f32[98,8,128]{2,1,0:T(8,128)S(1)} %get-tuple-element.10), channel_id=3, replica_groups={{0,16},{32,48},{64,80},{96,112},{128,144},{160,176},{192,208},{224,240}..., dimensions={0}, use_global_device_ids=true | all-gather | bytes 1204224 | tf_op jit(solution)/shard_map/all_gather | solution.py:296
  11.5 8.0 %all-gather.2 = f32[196,8,128]{2,1,0:T(8,128)S(1)} all-gather(f32[98,8,128]{2,1,0:T(8,128)S(1)} %get-tuple-element.11), channel_id=4, replica_groups={{16,32},{48,64},{80,96},{112,128},{144,160},{176,192},{208,224},{240,0}..., dimensions={0}, use_global_device_ids=true | all-gather | bytes 1204224 | tf_op jit(solution)/shard_map/all_gather | solution.py:297
  19.5 0.0 copy-done.5
  19.5 0.0 copy-start.1
  19.5 0.9 %shard_map.48 = (f32[98,32,128]{2,1,0:T(8,128)S(1)}, f32[7,32,128]{2,1,0:T(8,128)S(1)}, f32[7,32,128]{2,1,0:T(8,128)S(1)}) custom-call(f32[1,10,8,16,128]{4,3,2,1,0:T(8,128)S(1)} %copy-done, s32[1,8,16,128]{3,2,1,0:T(8,128)S(1)} %copy-done.2, s32[16,128]{1,0:T(8,128)S(1)} %copy-done.3, s32[16,128]{1,0:T(8,128)S(1)} %copy-done.5, ...), custom_call_target="tpu_custom_call" | custom-call | tf_op jit(solution)/shard_map/pallas_call | solution.py:280
  20.4 6.3 %all-gather.3 = f32[14,32,128]{2,1,0:T(8,128)S(1)} all-gather(f32[7,32,128]{2,1,0:T(8,128)S(1)} %get-tuple-element.16), channel_id=5, replica_groups={{0,1},{2,3},{4,5},{6,7},{8,9},{10,11},{12,13},{14,15},{16,17},{18,19},{..., dimensions={0}, use_global_device_ids=true | all-gather | bytes 344064 | tf_op jit(solution)/shard_map/all_gather | solution.py:304
  26.7 15.7 %all-gather.4 = f32[14,32,128]{2,1,0:T(8,128)S(1)} all-gather(f32[7,32,128]{2,1,0:T(8,128)S(1)} %get-tuple-element.15), channel_id=6, replica_groups={{1,2},{3,4},{5,6},{7,8},{9,10},{11,12},{13,14},{15,0},{17,18},{19,20},{..., dimensions={0}, use_global_device_ids=true | all-gather | bytes 344064 | tf_op jit(solution)/shard_map/all_gather | solution.py:305
  42.4 0.0 copy-done.1
  42.4 9.7 %shard_map.49 = f32[1,10,8,16,128]{4,3,2,1,0:T(8,128)} custom-call(f32[1,10,8,16,128]{4,3,2,1,0:T(8,128)S(1)} %copy-done.1, f32[98,32,128]{2,1,0:T(8,128)S(1)} %get-tuple-element.12.ext, f32[2,7,32,128]{3,2,1,0:T(8,128)S(1)} %bitcast.9, f32[2,7,32,128]{3,2,1,0:T(8,128)S(1)} %bitcast.10), custom_call_target="tpu_custom_call" | custom-call | tf_op jit(solution)/shard_map/pallas_call | solution.py:280
  (2 shorter events, 0.0 us)
Async XLA Ops:
  0.0 1.1 %copy-start = (f32[1,10,8,16,128]{4,3,2,1,0:T(8,128)S(1)}, f32[1,10,8,16,128]{4,3,2,1,0:T(8,128)}, u32[]{:S(2)}) copy-start(f32[1,10,8,16,128]{4,3,2,1,0:T(8,128)} %state.7) | copy-start | bytes 1966084
  6.9 0.8 %copy-start.2 = (s32[1,8,16,128]{3,2,1,0:T(8,128)S(1)}, s32[1,8,16,128]{3,2,1,0:T(8,128)}, u32[]{:S(2)}) copy-start(s32[1,8,16,128]{3,2,1,0:T(8,128)} %damage.3) | copy-start | bytes 196612
  7.7 0.7 %copy-start.3 = (s32[16,128]{1,0:T(8,128)S(1)}, s32[16,128]{1,0:T(8,128)}, u32[]{:S(2)}) copy-start(s32[16,128]{1,0:T(8,128)} %frame.3) | copy-start | bytes 24580
  8.4 0.7 %copy-start.4 = (s32[16,128]{1,0:T(8,128)S(1)}, s32[16,128]{1,0:T(8,128)}, u32[]{:S(2)}) copy-start(s32[16,128]{1,0:T(8,128)} %impact.3) | copy-start | bytes 24580
  9.1 10.4 %copy-start.5 = (s32[16,128]{1,0:T(8,128)S(1)}, s32[16,128]{1,0:T(8,128)}, u32[]{:S(2)}) copy-start(s32[16,128]{1,0:T(8,128)} %impact.3) | copy-start | bytes 24580
  19.5 22.9 %copy-start.1 = (f32[1,10,8,16,128]{4,3,2,1,0:T(8,128)S(1)}, f32[1,10,8,16,128]{4,3,2,1,0:T(8,128)}, u32[]{:S(2)}) copy-start(f32[1,10,8,16,128]{4,3,2,1,0:T(8,128)} %state.7) | copy-start | bytes 1966084

commit v2 on v1

--- a/solution.py
+++ b/solution.py
@@ -119,9 +119,8 @@
 
 
 def along_height(x):
-    a = x - lane_shift(x, -2)
-    b = 8.0 * a - lane_shift(a, 1)
-    return lane_shift(b, 1) - a
+    near = lane_shift(x, 1) - lane_shift(x, -1)
+    return 8.0 * near - (lane_shift(x, 2) - lane_shift(x, -2))
 
 
 def main_kernel(state, ext, near, far, out, fields, scale, extra):
@@ -142,8 +141,8 @@
     is_right = (lane < HALO) & has_right
     is_left = (lane >= LANES - HALO) & has_left
     for g in range(GROUPS):
-        from_right = jnp.where(odd == 0, near[1, g], far[1, g])
-        from_left = jnp.where(odd == 0, far[0, g], near[0, g])
+        from_right = jnp.where(odd == 0, near[1, g], far[g])
+        from_left = jnp.where(odd == 0, far[g], near[0, g])
         for j in range(min(PER_GROUP, PLANES - g * PER_GROUP)):
             plane = g * PER_GROUP + j
             r = pltpu.roll(from_right, LANES - HALO * j, 1) if j else from_right
@@ -187,7 +186,7 @@
             stiffness * (mate[3] - own[3]) + damping * (mate[2] - own[2]),
         ]
 
-        def body(z, carry):
+        def body(z):
             for v, a, b, c in ((VX, SXX, SXY, SXZ), (VY, SXY, SYY, SYZ), (VZ, SXZ, SYZ, SZZ)):
                 total = (
                     along_length(fields, spot(a, z), r0, n)
@@ -196,9 +195,9 @@
                 )
                 old = fields[spot(v, z), :, r0 : r0 + n, :]
                 fields[spot(v, z), :, r0 : r0 + n, :] = (old + step * total) * keep
-            return carry
-
-        lax.fori_loop(0, THICK, body, 0)
+
+        for z in range(THICK):
+            body(z)
         for f in range(3):
             at = spot(f, bonded)
             fields[at, :, r0 : r0 + n, :] += time_step * pull[f] * keep
@@ -251,25 +250,25 @@
 
     velocities(TOP - HALO, EXT, True)
 
-    def first_stress(z, carry):
+    def first_stress(z):
         r0, n = TOP - 4, ROWS + 8
         for f, change in enumerate(changes(z, r0, n, 2)):
             fields[spot(SXX + f, z), :, r0 : r0 + n, :] += change
         out[0, 9, z] = state[0, 9, z] + time_step * fields[spot(VZ, z), 0, TOP : TOP + ROWS, :]
-        return carry
-
-    lax.fori_loop(0, THICK, first_stress, 0)
+
+    for z in range(THICK):
+        first_stress(z)
     velocities(TOP - 4, ROWS + 8, False)
 
-    def last_stress(z, carry):
+    def last_stress(z):
         for f in range(3):
             out[0, f, z] = fields[spot(f, z), 0, TOP : TOP + ROWS, :]
         for f, change in enumerate(changes(z, TOP, ROWS, 1)):
             out[0, 3 + f, z] = fields[spot(SXX + f, z), 0, TOP : TOP + ROWS, :] + change[0]
         out[0, 9, z] += time_step * fields[spot(VZ, z), 0, TOP : TOP + ROWS, :]
-        return carry
-
-    lax.fori_loop(0, THICK, last_stress, 0)
+
+    for z in range(THICK):
+        last_stress(z)
 
 
 def shaped(*shape):
@@ -301,8 +300,9 @@
         local + (near, far),
     )
     even_place = lax.axis_index("hgt") % 2 == 0
+    swap = [(i, j) for pair in odd[:-1] for i, j in (pair, pair[::-1])]
+    far = lax.ppermute(jnp.where(even_place, left, right), "hgt", swap)
     near = lax.all_gather(jnp.where(even_place, right, left), "hgt", axis_index_groups=even)
-    far = lax.all_gather(jnp.where(even_place, left, right), "hgt", axis_index_groups=odd)
     return call(
         main_kernel,
         shaped(1, 10, THICK, ROWS, LANES),

time: 52.4 us -> 44.1 us (0.84)
  the two profiles are of different devices: /device:TPU:56 before, /device:TPU:6 now
where the time goes in v2:
time: 44.1 us; the launch traced here: 43.8 us
  blocking collectives  23.1 us (52%)
  starting transfers between devices  11.8 us (27%)
  Pallas kernels  5.48 us (12%)
  local copies, waits for them, and re-layouts  3.33 us (8%)
    ppermute x1, starting transfers between devices, per_device(): far = lax.ppermute(jnp.where(even_place, left, right), 'hgt', swap)  11.8 us
    all_gather x1, blocking collectives, per_device(): far = lax.all_gather(far, 'len', axis_index_groups=odd)  9.42 us
    all_gather x1, blocking collectives, per_device(): mate = lax.all_gather(surface, 'ply')  5.74 us
    pallas_call x4, Pallas kernels, call(): pl.pallas_call(kernel, out_shape=outs, in_specs=[VMEM] * len(args), out_s...  5.48 us
    all_gather x1, blocking collectives, per_device(): lax.all_gather(jnp.where(even_place, right, left), 'hgt', axis_index_grou...  5.47 us
    unnamed x16, local copies, waits for them, and re-layouts  3.33 us
    all_gather x1, blocking collectives, per_device(): near = lax.all_gather(near, 'len', axis_index_groups=even)  2.51 us
  transfers between devices with their start and end apart: 1, of which 0 were waited for; matrix products, arithmetic and copies ran while one was open for 0% of the time, Pallas kernels for 0%

profile of v2, /device:TPU:6, one launch (start us, length us, event | category | flops | bytes accessed | tf_op | source)
XLA Modules:
  0.0 43.8 jit_solution(9511155307989487312)
XLA Ops:
  0.0 0.0 copy-start
  0.0 1.1 %copy-done = f32[1,10,8,16,128]{4,3,2,1,0:T(8,128)S(1)} copy-done((f32[1,10,8,16,128]{4,3,2,1,0:T(8,128)S(1)}, f32[1,10,8,16,128]{4,3,2,1,0:T(8,128)}, u32[]{:S(2)}) %copy-start) | copy-done | bytes 655384
  1.1 5.7 %all-gather = f32[30,16,128]{2,1,0:T(8,128)S(1)} all-gather(f32[15,16,128]{2,1,0:T(8,128)S(1)} %shard_map.46), channel_id=2, replica_groups=mesh['ply'=2,'len'=16,'hgt'=16] {'ply'}, dimensions={0}, use_global_device_ids=true | all-gather | bytes 368640 | tf_op jit(solution)/shard_map/all_gather | solution.py:292
  6.9 0.0 copy-start.2
  6.9 0.8 %copy-done.2 = s32[1,8,16,128]{3,2,1,0:T(8,128)S(1)} copy-done((s32[1,8,16,128]{3,2,1,0:T(8,128)S(1)}, s32[1,8,16,128]{3,2,1,0:T(8,128)}, u32[]{:S(2)}) %copy-start.2) | copy-done | bytes 65560
  7.7 0.0 copy-start.4
  7.7 0.7 %copy-done.4 = s32[16,128]{1,0:T(8,128)S(1)} copy-done((s32[16,128]{1,0:T(8,128)S(1)}, s32[16,128]{1,0:T(8,128)}, u32[]{:S(2)}) %copy-start.4) | copy-done | bytes 8216
  8.4 0.7 %copy-done.6 = s32[16,128]{1,0:T(8,128)S(1)} copy-done((s32[16,128]{1,0:T(8,128)S(1)}, s32[16,128]{1,0:T(8,128)}, u32[]{:S(2)}) %copy-start.6) | copy-done | bytes 8216
  9.1 0.0 copy-start.1
  9.1 0.0 copy-start.3
  9.1 0.0 copy-start.5
  9.1 0.0 copy-start.7
  9.1 0.1 shard_map.47
  9.2 2.5 %all-gather.1 = f32[196,8,128]{2,1,0:T(8,128)S(1)} all-gather(f32[98,8,128]{2,1,0:T(8,128)S(1)} %get-tuple-element.10), channel_id=3, replica_groups={{0,16},{32,48},{64,80},{96,112},{128,144},{160,176},{192,208},{224,240}..., dimensions={0}, use_global_device_ids=true | all-gather | bytes 1204224 | tf_op jit(solution)/shard_map/all_gather | solution.py:295
  11.7 9.4 %all-gather.2 = f32[196,8,128]{2,1,0:T(8,128)S(1)} all-gather(f32[98,8,128]{2,1,0:T(8,128)S(1)} %get-tuple-element.11), channel_id=4, replica_groups={{16,32},{48,64},{80,96},{112,128},{144,160},{176,192},{208,224},{240,0}..., dimensions={0}, use_global_device_ids=true | all-gather | bytes 1204224 | tf_op jit(solution)/shard_map/all_gather | solution.py:296
  21.1 0.0 copy-done.1
  21.1 0.0 copy-done.3
  21.1 0.0 copy-done.5
  21.1 0.0 copy-done.7
  21.1 0.9 %shard_map.48 = (f32[98,32,128]{2,1,0:T(8,128)S(1)}, f32[7,32,128]{2,1,0:T(8,128)S(1)}, f32[7,32,128]{2,1,0:T(8,128)S(1)}) custom-call(f32[1,10,8,16,128]{4,3,2,1,0:T(8,128)S(1)} %copy-done.1, s32[1,8,16,128]{3,2,1,0:T(8,128)S(1)} %copy-done.3, s32[16,128]{1,0:T(8,128)S(1)} %copy-done.5, s32[16,128]{1,0:T(8,128)S(1)} %copy-done.7, ...), custom_call_target="tpu_custom_call" | custom-call | tf_op jit(solution)/shard_map/pallas_call | solution.py:279
  22.1 11.8 %collective-permute-start = (f32[7,32,128]{2,1,0:T(8,128)S(1)}, f32[7,32,128]{2,1,0:T(8,128)S(1)}, u32[]{:S(2)}, u32[]{:S(2)}) collective-permute-start(f32[7,32,128]{2,1,0:T(8,128)S(1)} %get-tuple-element.15), channel_id=1, source_target_pairs={{1,2},{2,1},{3,4},{4,3},{5,6},{6,5},{7,8},{8,7},{9,10},{10,9},{11,... | collective-permute-start | bytes 344072 | tf_op jit(solution)/shard_map/ppermute | solution.py:304
  33.9 5.5 %all-gather.3 = f32[14,32,128]{2,1,0:T(8,128)S(1)} all-gather(f32[7,32,128]{2,1,0:T(8,128)S(1)} %get-tuple-element.16), channel_id=5, replica_groups={{0,1},{2,3},{4,5},{6,7},{8,9},{10,11},{12,13},{14,15},{16,17},{18,19},{..., dimensions={0}, use_global_device_ids=true | all-gather | bytes 344064 | tf_op jit(solution)/shard_map/all_gather | solution.py:305
  39.3 0.0 collective-permute-done.far
  39.3 4.5 %shard_map.49 = f32[1,10,8,16,128]{4,3,2,1,0:T(8,128)} custom-call(f32[1,10,8,16,128]{4,3,2,1,0:T(8,128)S(1)} %copy-done.1, f32[98,32,128]{2,1,0:T(8,128)S(1)} %get-tuple-element.12.ext, f32[2,7,32,128]{3,2,1,0:T(8,128)S(1)} %bitcast.8, f32[7,32,128]{2,1,0:T(8,128)S(1)} %collective-permute-done.far), custom_call_target="tpu_custom_call" | custom-call | tf_op jit(solution)/shard_map/pallas_call | solution.py:279
  (3 shorter events, 0.0 us)
Async XLA Ops:
  0.0 1.1 %copy-start = (f32[1,10,8,16,128]{4,3,2,1,0:T(8,128)S(1)}, f32[1,10,8,16,128]{4,3,2,1,0:T(8,128)}, u32[]{:S(2)}) copy-start(f32[1,10,8,16,128]{4,3,2,1,0:T(8,128)} %state.7) | copy-start | bytes 1966084
  6.9 0.8 %copy-start.2 = (s32[1,8,16,128]{3,2,1,0:T(8,128)S(1)}, s32[1,8,16,128]{3,2,1,0:T(8,128)}, u32[]{:S(2)}) copy-start(s32[1,8,16,128]{3,2,1,0:T(8,128)} %damage.3) | copy-start | bytes 196612
  7.7 0.7 %copy-start.4 = (s32[16,128]{1,0:T(8,128)S(1)}, s32[16,128]{1,0:T(8,128)}, u32[]{:S(2)}) copy-start(s32[16,128]{1,0:T(8,128)} %frame.3) | copy-start | bytes 24580
  8.4 0.7 %copy-start.6 = (s32[16,128]{1,0:T(8,128)S(1)}, s32[16,128]{1,0:T(8,128)}, u32[]{:S(2)}) copy-start(s32[16,128]{1,0:T(8,128)} %impact.3) | copy-start | bytes 24580
  9.1 12.0 %copy-start.1 = (f32[1,10,8,16,128]{4,3,2,1,0:T(8,128)S(1)}, f32[1,10,8,16,128]{4,3,2,1,0:T(8,128)}, u32[]{:S(2)}) copy-start(f32[1,10,8,16,128]{4,3,2,1,0:T(8,128)} %state.7) | copy-start | bytes 1966084
  9.1 12.0 %copy-start.3 = (s32[1,8,16,128]{3,2,1,0:T(8,128)S(1)}, s32[1,8,16,128]{3,2,1,0:T(8,128)}, u32[]{:S(2)}) copy-start(s32[1,8,16,128]{3,2,1,0:T(8,128)} %damage.3) | copy-start | bytes 196612
  9.1 12.0 %copy-start.5 = (s32[16,128]{1,0:T(8,128)S(1)}, s32[16,128]{1,0:T(8,128)}, u32[]{:S(2)}) copy-start(s32[16,128]{1,0:T(8,128)} %frame.3) | copy-start | bytes 24580
  9.1 12.0 %copy-start.7 = (s32[16,128]{1,0:T(8,128)S(1)}, s32[16,128]{1,0:T(8,128)}, u32[]{:S(2)}) copy-start(s32[16,128]{1,0:T(8,128)} %impact.3) | copy-start | bytes 24580
  22.1 17.3 %collective-permute-start = (f32[7,32,128]{2,1,0:T(8,128)S(1)}, f32[7,32,128]{2,1,0:T(8,128)S(1)}, u32[]{:S(2)}, u32[]{:S(2)}) collective-permute-start(f32[7,32,128]{2,1,0:T(8,128)S(1)} %get-tuple-element.15), channel_id=1, source_target_pairs={{1,2},{2,1},{3,4},{4,3},{5,6},{6,5},{7,8},{8,7},{9,10},{10,9},{11,... | collective-permute-start | bytes 344072 | tf_op jit(solution)/shard_map/ppermute | solution.py:304

commit v3 on v0

v3 whole, which is shorter than its diff:
```python
import jax
import jax.numpy as jnp
from jax import lax
from jax.experimental import pallas as pl
from jax.experimental.pallas import tpu as pltpu
from jax.sharding import PartitionSpec as P

time_step = 0.25
softening = 0.15
damping = 1.0
stiffness = 2.0
pressure = 2.0

THICK = 8
ROWS = 16
LANES = 128
HALO = 8
STEP = time_step / 12.0

VX, VY, VZ, SXX, SYY, SZZ, SXY, SXZ, SYZ, SCALE = range(10)
DISP, KEEP, PUSH, OWN = 80, 81, 82, 83
DISP_ALL = 83
MATE = 83
ALL = 98
M_VX, M_VY, M_VZ, M_W, M_XX, M_YY, M_XY, M_XZ, M_YZ = range(MATE, MATE + 9)
M_XZ1, M_YZ1, M_ZZ1, M_XZ2, M_YZ2, M_ZZ2 = range(MATE + 9, MATE + 15)

PER_GROUP = 16
GROUPS = 6
MATE_SENT = 17

VMEM = pl.BlockSpec(memory_space=pltpu.VMEM)
MIB = 2**20


def at(field, z):
    return field * THICK + z


def fours():
    items = [(at(f, z), False) for f in (SXX, SXY, SXZ, SCALE) for z in range(THICK)]
    items += [(at(f, z), True) for f in (VX, VY, VZ) for z in range(THICK)]
    return items + [(p, False) for p in (M_XX, M_XY, M_XZ)]


def twos():
    items = [at(f, z) for f in (SYY, SZZ, SYZ, VX, VY, VZ) for z in range(THICK)]
    items += [M_VX, M_VY, M_VZ, M_W, M_YY, M_YZ, M_XZ1, M_YZ1, M_ZZ1, M_XZ2, M_YZ2, M_ZZ2]
    return items + [DISP, KEEP, PUSH]


def travel(down):
    moves, row = [], 0
    for plane, new in fours():
        first = (10 if new else 12) if down else (2 if new else 0)
        moves.append((plane, first, 4, new, row // 8, row % 8))
        row += 4
    for plane in twos():
        moves.append((plane, 14 if down else 0, 2, False, row // 8, row % 8))
        row += 2
    return moves


SENT = -(-(4 * len(fours()) + 2 * len(twos())) // 8)
SENT_SIDES = -(-SENT // 8)
SENT_ALL = SENT + SENT_SIDES


def lanes_of(rows):
    return lax.broadcasted_iota(jnp.int32, (rows, LANES), 1)


def turn(x, by):
    by %= LANES
    return pltpu.roll(x, by, 1) if by else x


def pack_sides(planes):
    slot = lanes_of(planes[0].shape[0]) // 16
    packed = jnp.zeros(planes[0].shape, jnp.float32)
    for j, plane in enumerate(planes):
        packed = jnp.where(slot == j, turn(plane, HALO + 16 * j), packed)
    return packed


def unpack_side(packed, j):
    lane = lanes_of(packed.shape[0])
    side = turn(packed, -(HALO + 16 * j))
    return jnp.where((lane < HALO) | (lane >= LANES - HALO), side, 0.0)


def lane_shift(x, s):
    lane = lax.broadcasted_iota(jnp.int32, x.shape, 2)
    turned = pltpu.roll(x, (-s) % LANES, 2)
    other = jnp.concatenate([turned[1:2], turned[0:1]], axis=0)
    inside = lane < LANES - s if s > 0 else lane >= -s
    return jnp.where(inside, turned, other)


def along_height(x):
    near = lane_shift(x, 1) - lane_shift(x, -1)
    return 8.0 * near - (lane_shift(x, 2) - lane_shift(x, -2))


def along_length(look, plane, r0, n):
    near = look(plane, r0 + 1, n) - look(plane, r0 - 1, n)
    return 8.0 * near - (look(plane, r0 + 2, n) - look(plane, r0 - 2, n))


def through(look, field, z, r0, n):
    def layer(k):
        return look(at(field, k), r0, n) if 0 <= k < THICK else jnp.zeros((2, n, LANES), jnp.float32)

    return 8.0 * (layer(z + 1) - layer(z - 1)) - (layer(z + 2) - layer(z - 2))


def new_velocities(look, r0, n, front, put, with_mate):
    keep = look(KEEP, r0, n)

    def bonded(field):
        return jnp.where(front, look(at(field, THICK - 1), r0, n), look(at(field, 0), r0, n))

    mate = [look(p, r0, n) for p in (M_VX, M_VY, M_VZ, M_W)]
    pull = [
        damping * (mate[0] - bonded(VX)),
        damping * (mate[1] - bonded(VY)),
        stiffness * (mate[3] - look(DISP, r0, n)) + damping * (mate[2] - bonded(VZ)),
    ]
    pull = [time_step * p for p in pull]
    push = jnp.where(front, time_step * pressure, 0.0) * look(PUSH, r0, n)
    if with_mate:
        sign = jnp.where(front, 1.0, -1.0)
        parts = ((M_XX, M_XY, M_XZ1, M_XZ2), (M_XY, M_YY, M_YZ1, M_YZ2), (M_XZ, M_YZ, M_ZZ1, M_ZZ2))
        for f, (a, b, one, two) in enumerate(parts):
            total = (
                along_length(look, a, r0, n)
                + along_height(look(b, r0, n))
                + sign * (8.0 * look(one, r0, n) - look(two, r0, n))
            )
            put(M_VX + f, (mate[f] + STEP * total - pull[f]) * keep)
    for z in range(THICK):
        for f, (a, b, c) in enumerate(((SXX, SXY, SXZ), (SXY, SYY, SYZ), (SXZ, SYZ, SZZ))):
            total = (
                along_length(look, at(a, z), r0, n)
                + along_height(look(at(b, z), r0, n))
                + through(look, c, z, r0, n)
            )
            fresh = look(at(f, z), r0, n) + STEP * total
            if z == 0:
                fresh += jnp.where(front, 0.0, 1.0) * pull[f]
                if f == 2:
                    fresh += push
            if z == THICK - 1:
                fresh += jnp.where(front, 1.0, 0.0) * pull[f]
            put(at(f, z), fresh * keep)


def fetch_kernel(state, damage, frame, impact, tile, near, far, levels, held, struck, arrived):
    copies = [
        pltpu.make_async_copy(damage.at[0], levels, arrived.at[10]),
        pltpu.make_async_copy(frame, held, arrived.at[11]),
        pltpu.make_async_copy(impact, struck, arrived.at[12]),
    ]
    for f in range(10):
        first = DISP_ALL if f == 9 else at(f, 0)
        copies.append(
            pltpu.make_async_copy(state.at[0, f], tile.at[pl.ds(first, THICK)], arrived.at[f])
        )
    for copy in copies:
        copy.start()
    for copy in copies:
        copy.wait()
    front = lax.axis_index("ply") == 0
    even = lax.axis_index("hgt") % 2 == 0
    for z in range(THICK):
        tile[at(SCALE, z)] = 1.0 - softening * levels[z].astype(jnp.float32)
    tile[DISP] = jnp.where(front, tile[DISP_ALL + THICK - 1], tile[DISP_ALL])
    tile[KEEP] = (1 - held[...]).astype(jnp.float32)
    tile[PUSH] = struck[...].astype(jnp.float32)
    slot = lanes_of(ROWS) // HALO
    for g in range(GROUPS):
        first = jnp.zeros((ROWS, LANES), jnp.float32)
        last = first
        for j in range(min(PER_GROUP, OWN - g * PER_GROUP)):
            plane = tile[g * PER_GROUP + j]
            first = jnp.where(slot == j, turn(plane, HALO * j), first)
            last = jnp.where(slot == j, turn(plane, HALO * j + HALO), last)
        near[g] = jnp.where(even, last, first)
        far[g] = jnp.where(even, first, last)


def side_kernel(tile, near, far, side, surface):
    front = lax.axis_index("ply") == 0
    place = lax.axis_index("hgt")
    even = place % 2 == 0
    lane = lanes_of(ROWS)
    is_right = (lane < HALO) & (place < lax.axis_size("hgt") - 1)
    is_left = (lane >= LANES - HALO) & (place > 0)
    for g in range(GROUPS):
        from_right = jnp.where(even, near[1, g], far[g])
        from_left = jnp.where(even, far[g], near[0, g])
        for j in range(min(PER_GROUP, OWN - g * PER_GROUP)):
            r = turn(from_right, -HALO * j)
            m = turn(from_left, -HALO - HALO * j)
            side[g * PER_GROUP + j] = jnp.where(is_right, r, jnp.where(is_left, m, 0.0))
    picks = [(VX, 0), (VY, 0), (VZ, 0), None, (SXX, 0), (SYY, 0), (SXY, 0), (SXZ, 0), (SYZ, 0)]
    picks += [(f, depth) for depth in (1, 2) for f in (SXZ, SYZ, SZZ)]
    sides = []
    for k, pick in enumerate(picks):
        if pick is None:
            surface[k] = tile[DISP]
            sides.append(side[DISP])
        else:
            low, high = at(pick[0], pick[1]), at(pick[0], THICK - 1 - pick[1])
            surface[k] = jnp.where(front, tile[high], tile[low])
            sides.append(jnp.where(front, side[high], side[low]))
    surface[15] = pack_sides(sides[:8])
    surface[16] = pack_sides(sides[8:])


def speed_kernel(tile, side, mates, fresh, mate, near, far, middle, flank):
    front = lax.axis_index("ply") == 0
    core = lax.axis_index("len") % 2
    other = jnp.where(front, 1, 0)
    for k in range(15):
        mate[k, 0] = mates[other, k]
        mate[k, 1] = unpack_side(mates[other, 15 + k // 8], k % 8)

    def look(plane, r, n):
        if plane >= MATE:
            return mate[plane - MATE, :, r : r + n, :]
        return jnp.stack([tile[plane, r : r + n, :], side[plane, r : r + n, :]])

    def put(plane, value):
        fresh[plane if plane < 24 else 24 + plane - MATE, :, 2 : ROWS - 2, :] = value

    new_velocities(look, 2, ROWS - 4, front, put, True)

    for down in (0, 1):
        middle[down, SENT - 1] = jnp.zeros((HALO, LANES), jnp.float32)
        flank[down, SENT - 1] = jnp.zeros((HALO, LANES), jnp.float32)
        for plane, r, n, new, k, row in travel(down):
            value = fresh[plane, :, r : r + n, :] if new else look(plane, r, n)
            middle[down, k, row : row + n, :] = value[0]
            flank[down, k, row : row + n, :] = value[1]
    for out, way in ((near, 1 - core), (far, core)):
        for k in range(SENT):
            out[k] = middle[way, k]
        for g in range(SENT_SIDES):
            ks = range(8 * g, min(8 * g + 8, SENT))
            out[SENT + g] = pack_sides([flank[way, k] for k in ks])


def last_kernel(tile, side, fresh, mate, near, far, out, cells):
    front = lax.axis_index("ply") == 0
    index = lax.axis_index("len")
    upper = index % 2 == 0
    has_top = index > 0
    has_bottom = index < lax.axis_size("len") - 1

    for plane in range(OWN):
        cells[plane, 0, HALO : HALO + ROWS, :] = tile[plane]
        cells[plane, 1, HALO : HALO + ROWS, :] = side[plane]
    for k in range(15):
        cells[MATE + k, :, HALO : HALO + ROWS, :] = mate[k]
    for k in range(27):
        plane = k if k < 24 else MATE + k - 24
        cells[plane, :, HALO + 2 : HALO + ROWS - 2, :] = fresh[k, :, 2 : ROWS - 2, :]
    for down, there in ((1, has_top), (0, has_bottom)):

        def sent(k):
            first, second = (far[0, k], near[0, k]) if down else (near[1, k], far[1, k])
            return jnp.where(there, jnp.where(upper, first, second), 0.0)

        packed = [sent(SENT + g) for g in range(SENT_SIDES)]
        move = -ROWS if down else ROWS
        held = None
        for plane, r, n, _, k, row in travel(down):
            if k != held:
                held, main, flank = k, sent(k), unpack_side(packed[k // 8], k % 8)
            place = HALO + r + move
            cells[plane, 0, place : place + n, :] = main[row : row + n]
            cells[plane, 1, place : place + n, :] = flank[row : row + n]

    def look(plane, r, n):
        return cells[plane, :, HALO + r : HALO + r + n, :]

    def writer(r, n):
        def put(plane, value):
            cells[plane, :, HALO + r : HALO + r + n, :] = value

        return put

    for r in (-2, ROWS - 2):
        new_velocities(look, r, 4, front, writer(r, 4), True)
    r, n = -2, ROWS + 4
    put = writer(r, n)
    own_z = jnp.where(front, look(at(VZ, THICK - 1), r, n), look(at(VZ, 0), r, n))
    put(DISP, look(DISP, r, n) + time_step * own_z)
    put(M_W, look(M_W, r, n) + time_step * look(M_VZ, r, n))

    def changes(z, r, n, size):
        def length_of(f):
            return along_length(look, at(f, z), r, n)[:size]

        def height_of(f):
            return along_height(look(at(f, z), r, n))[:size]

        def depth_of(f):
            return through(look, f, z, r, n)[:size]

        factor = STEP * look(at(SCALE, z), r, n)[:size]
        xx, yy, zz = length_of(VX), height_of(VY), depth_of(VZ)
        whole = xx + yy + zz
        return (
            factor * (whole + 2.0 * xx),
            factor * (whole + 2.0 * yy),
            factor * (whole + 2.0 * zz),
            factor * (height_of(VX) + length_of(VY)),
            factor * (depth_of(VX) + length_of(VZ)),
            factor * (depth_of(VY) + height_of(VZ)),
        )

    r, n = -4, ROWS + 8
    put = writer(r, n)
    for z in range(THICK):
        for f, change in enumerate(changes(z, r, n, 2)):
            put(at(SXX + f, z), look(at(SXX + f, z), r, n) + change)
        out[0, 9, z] = tile[DISP_ALL + z] + time_step * look(at(VZ, z), 0, ROWS)[0]
    new_velocities(look, -2, ROWS + 4, front, writer(-2, ROWS + 4), False)
    for z in range(THICK):
        for f in range(3):
            out[0, f, z] = look(at(f, z), 0, ROWS)[0]
        for f, change in enumerate(changes(z, 0, ROWS, 1)):
            out[0, 3 + f, z] = look(at(SXX + f, z), 0, ROWS)[0] + change[0]
        out[0, 9, z] += time_step * look(at(VZ, z), 0, ROWS)[0]


def shaped(*shape):
    return jax.ShapeDtypeStruct(shape, jnp.float32)


def call(kernel, outs, args, limit=32 * MIB, space=pltpu.VMEM, scratch=()):
    return pl.pallas_call(
        kernel,
        out_shape=outs,
        in_specs=[pl.BlockSpec(memory_space=space)] * len(args),
        out_specs=jax.tree.map(lambda _: VMEM, outs),
        scratch_shapes=scratch,
        compiler_params=pltpu.CompilerParams(vmem_limit_bytes=limit),
    )(*args)


FETCH_LIMIT = 32 * MIB


def per_device(plate_state, damage, frame_mask, impact_mask):
    even = [[2 * i, 2 * i + 1] for i in range(8)]
    odd = [[2 * i + 1, (2 * i + 2) % 16] for i in range(8)]
    strips = shaped(GROUPS, ROWS, LANES)
    tile, near, far = call(
        fetch_kernel,
        [shaped(OWN + THICK, ROWS, LANES), strips, strips],
        (plate_state, damage, frame_mask, impact_mask),
        limit=FETCH_LIMIT,
        space=pl.ANY,
        scratch=[
            pltpu.VMEM((THICK, ROWS, LANES), jnp.int32),
            pltpu.VMEM((ROWS, LANES), jnp.int32),
            pltpu.VMEM((ROWS, LANES), jnp.int32),
            pltpu.SemaphoreType.DMA((13,)),
        ],
    )
    swap = [(i, j) for pair in odd[:-1] for i, j in (pair, pair[::-1])]
    far = lax.ppermute(far, "hgt", swap)
    near = lax.all_gather(near, "hgt", axis_index_groups=even)
    side, surface = call(
        side_kernel,
        [shaped(OWN, ROWS, LANES), shaped(MATE_SENT, ROWS, LANES)],
        (tile, near, far),
    )
    mates = lax.all_gather(surface, "ply")
    sent = shaped(SENT_ALL, HALO, LANES)
    fresh, mate, near, far = call(
        speed_kernel,
        [shaped(27, 2, ROWS, LANES), shaped(15, 2, ROWS, LANES), sent, sent],
        (tile, side, mates),
        scratch=[pltpu.VMEM((2, SENT, HALO, LANES), jnp.float32)] * 2,
    )
    near = lax.all_gather(near, "len", axis_index_groups=even)
    far = lax.all_gather(far, "len", axis_index_groups=odd)
    return call(
        last_kernel,
        shaped(1, 10, THICK, ROWS, LANES),
        (tile, side, fresh, mate, near, far),
        scratch=[pltpu.VMEM((ALL, 2, ROWS + 2 * HALO, LANES), jnp.float32)],
    )


def solution(mesh):
    placed = (
        P("ply", None, None, "len", "hgt"),
        P("ply", None, "len", "hgt"),
        P("len", "hgt"),
        P("len", "hgt"),
    )
    return jax.shard_map(
        per_device,
        mesh=mesh,
        in_specs=placed,
        out_specs=P("ply", None, None, "len", "hgt"),
        check_vma=False,
    )
```

time: 112 us -> 41.6 us (0.37)
  starting transfers between devices: 76.6 us -> 11.5 us
  blocking collectives: 0 us -> 20.3 us
  waiting for transfers between devices: 17.8 us -> 0.01 us
  local copies, waits for them, and re-layouts: 10.9 us -> 3.32 us
  Pallas kernels: 0 us -> 6.13 us
  other arithmetic: 5.26 us -> 0 us
    ppermute x18 -> x1, starting transfers between devices: 76.6 us -> 11.5 us  [per_device(): far = lax.ppermute(far, 'hgt', swap)]
    all_gather x0 -> x4, blocking collectives: none -> 20.3 us  [the longest x1 7.15 us: per_device(): far = lax.all_gather(far, 'len', axis_index_groups=odd)]
    ppermute x18 -> x1, waiting for transfers between devices: 17.8 us -> 0.01 us  [per_device(): far = lax.ppermute(far, 'hgt', swap)]
    slice x46 -> x0, local copies, waits for them, and re-layouts: 6.36 us -> none  [the longest x22 1.9 us: shifted(): return lax.slice_in_dim(field, 2 + offset, 2 + offset + count, axis=axis)]
    pallas_call x0 -> x4, Pallas kernels: none -> 6.13 us  [call(): pl.pallas_call(kernel, out_shape=outs, in_specs=[pl.BlockSpec(memory_spac...]
    ppermute x4 -> x0, local copies, waits for them, and re-layouts: 1.63 us -> none  [the longest x2 0.82 us: padded_2(): lax.ppermute(tail, axis, [(i, (i + 1) % count) for i in range(ends)])]
    concatenate x8 -> x0, other arithmetic: 1.53 us -> none  [padded_2(): jnp.concatenate([lax.ppermute(tail, axis, [(i, (i + 1) % count) for i in...]
    unnamed x12 -> x8, local copies, waits for them, and re-layouts: 2.49 us -> 3.32 us
  transfers between devices with their start and end apart: 18 -> 1, of which waited for: 9 -> 0; matrix products, arithmetic and copies ran while one was open for 5% -> 0% of each run, Pallas kernels for 0% -> 0%
where the time goes in v3:
time: 41.6 us; the launch traced here: 41.3 us
  blocking collectives  20.3 us (49%)
  starting transfers between devices  11.5 us (28%)
  Pallas kernels  6.13 us (15%)
  local copies, waits for them, and re-layouts  3.32 us (8%)
    ppermute x1, starting transfers between devices, per_device(): far = lax.ppermute(far, 'hgt', swap)  11.5 us
    all_gather x1, blocking collectives, per_device(): far = lax.all_gather(far, 'len', axis_index_groups=odd)  7.15 us
    pallas_call x4, Pallas kernels, call(): pl.pallas_call(kernel, out_shape=outs, in_specs=[pl.BlockSpec(memory_spac...  6.13 us
    all_gather x1, blocking collectives, per_device(): near = lax.all_gather(near, 'len', axis_index_groups=even)  4.99 us
    all_gather x1, blocking collectives, per_device(): mates = lax.all_gather(surface, 'ply')  4.58 us
    all_gather x1, blocking collectives, per_device(): near = lax.all_gather(near, 'hgt', axis_index_groups=even)  3.62 us
    unnamed x8, local copies, waits for them, and re-layouts  3.32 us
  transfers between devices with their start and end apart: 1, of which 0 were waited for; matrix products, arithmetic and copies ran while one was open for 0% of the time, Pallas kernels for 0%

profile of v3, /device:TPU:31, one launch (start us, length us, event | category | flops | bytes accessed | tf_op | source)
XLA Modules:
  0.0 41.3 jit_solution(1017972109525112046)
XLA Ops:
  0.0 0.0 copy-start
  0.0 1.1 %copy-done = f32[1,10,8,16,128]{4,3,2,1,0:T(8,128)S(1)} copy-done((f32[1,10,8,16,128]{4,3,2,1,0:T(8,128)S(1)}, f32[1,10,8,16,128]{4,3,2,1,0:T(8,128)}, u32[]{:S(2)}) %copy-start) | copy-done | bytes 655384
  1.1 0.0 copy-start.1
  1.1 0.8 %copy-done.1 = s32[1,8,16,128]{3,2,1,0:T(8,128)S(1)} copy-done((s32[1,8,16,128]{3,2,1,0:T(8,128)S(1)}, s32[1,8,16,128]{3,2,1,0:T(8,128)}, u32[]{:S(2)}) %copy-start.1) | copy-done | bytes 65560
  1.9 0.0 copy-start.2
  1.9 0.7 %copy-done.2 = s32[16,128]{1,0:T(8,128)S(1)} copy-done((s32[16,128]{1,0:T(8,128)S(1)}, s32[16,128]{1,0:T(8,128)}, u32[]{:S(2)}) %copy-start.2) | copy-done | bytes 8216
  2.6 0.0 copy-start.3
  2.6 0.7 %copy-done.3 = s32[16,128]{1,0:T(8,128)S(1)} copy-done((s32[16,128]{1,0:T(8,128)S(1)}, s32[16,128]{1,0:T(8,128)}, u32[]{:S(2)}) %copy-start.3) | copy-done | bytes 8216
  3.3 1.4 %shard_map.46 = (f32[91,16,128]{2,1,0:T(8,128)S(1)}, f32[6,16,128]{2,1,0:T(8,128)S(1)}, f32[6,16,128]{2,1,0:T(8,128)S(1)}) custom-call(f32[1,10,8,16,128]{4,3,2,1,0:T(8,128)S(1)} %copy-done, s32[1,8,16,128]{3,2,1,0:T(8,128)S(1)} %copy-done.1, s32[16,128]{1,0:T(8,128)S(1)} %copy-done.2, s32[16,128]{1,0:T(8,128)S(1)} %copy-done.3), custom_call_target="tpu_custom_call" | custom-call | tf_op jit(solution)/shard_map/pallas_call | solution.py:344
  4.8 11.5 %collective-permute-start = (f32[6,16,128]{2,1,0:T(8,128)S(1)}, f32[6,16,128]{2,1,0:T(8,128)S(1)}, u32[]{:S(2)}, u32[]{:S(2)}) collective-permute-start(f32[6,16,128]{2,1,0:T(8,128)S(1)} %get-tuple-element.16), channel_id=1, source_target_pairs={{1,2},{2,1},{3,4},{4,3},{5,6},{6,5},{7,8},{8,7},{9,10},{10,9},{11,... | collective-permute-start | bytes 147464 | tf_op jit(solution)/shard_map/ppermute | solution.py:375
  16.3 3.6 %all-gather = f32[12,16,128]{2,1,0:T(8,128)S(1)} all-gather(f32[6,16,128]{2,1,0:T(8,128)S(1)} %get-tuple-element.15), channel_id=2, replica_groups={{0,1},{2,3},{4,5},{6,7},{8,9},{10,11},{12,13},{14,15},{16,17},{18,19},{..., dimensions={0}, use_global_device_ids=true | all-gather | bytes 147456 | tf_op jit(solution)/shard_map/all_gather | solution.py:376
  19.9 0.0 collective-permute-done.far
  19.9 0.5 %shard_map.47 = (f32[83,16,128]{2,1,0:T(8,128)S(1)}, f32[17,16,128]{2,1,0:T(8,128)S(1)}) custom-call(f32[91,16,128]{2,1,0:T(8,128)S(1)} %get-tuple-element.14.tile, f32[2,6,16,128]{3,2,1,0:T(8,128)S(1)} %bitcast.7, f32[6,16,128]{2,1,0:T(8,128)S(1)} %collective-permute-done.far), custom_call_target="tpu_custom_call" | custom-call | tf_op jit(solution)/shard_map/pallas_call | solution.py:344
  20.4 4.6 %all-gather.1 = f32[34,16,128]{2,1,0:T(8,128)S(1)} all-gather(f32[17,16,128]{2,1,0:T(8,128)S(1)} %get-tuple-element.18), channel_id=3, replica_groups=mesh['ply'=2,'len'=16,'hgt'=16] {'ply'}, dimensions={0}, use_global_device_ids=true | all-gather | bytes 417792 | tf_op jit(solution)/shard_map/all_gather | solution.py:382
  25.0 0.9 %shard_map.48 = (f32[27,2,16,128]{3,2,1,0:T(8,128)S(1)}, f32[15,2,16,128]{3,2,1,0:T(8,128)S(1)}, f32[52,8,128]{2,1,0:T(8,128)S(1)}, f32[52,8,128]{2,1,0:T(8,128)S(1)}) custom-call(f32[91,16,128]{2,1,0:T(8,128)S(1)} %get-tuple-element.14.tile, f32[83,16,128]{2,1,0:T(8,128)S(1)} %get-tuple-element.17.side, f32[2,17,16,128]{3,2,1,0:T(8,128)S(1)} %bitcast.6), custom_call_target="tpu_custom_call" | custom-call | tf_op jit(solution)/shard_map/pallas_call | solution.py:344
  25.8 5.0 %all-gather.2 = f32[104,8,128]{2,1,0:T(8,128)S(1)} all-gather(f32[52,8,128]{2,1,0:T(8,128)S(1)} %get-tuple-element.21), channel_id=4, replica_groups={{0,16},{32,48},{64,80},{96,112},{128,144},{160,176},{192,208},{224,240}..., dimensions={0}, use_global_device_ids=true | all-gather | bytes 638976 | tf_op jit(solution)/shard_map/all_gather | solution.py:390
  30.8 7.1 %all-gather.3 = f32[104,8,128]{2,1,0:T(8,128)S(1)} all-gather(f32[52,8,128]{2,1,0:T(8,128)S(1)} %get-tuple-element.22), channel_id=5, replica_groups={{16,32},{48,64},{80,96},{112,128},{144,160},{176,192},{208,224},{240,0}..., dimensions={0}, use_global_device_ids=true | all-gather | bytes 638976 | tf_op jit(solution)/shard_map/all_gather | solution.py:391
  38.0 3.4 %shard_map.49 = f32[1,10,8,16,128]{4,3,2,1,0:T(8,128)} custom-call(f32[91,16,128]{2,1,0:T(8,128)S(1)} %get-tuple-element.14.tile, f32[83,16,128]{2,1,0:T(8,128)S(1)} %get-tuple-element.17.side, f32[27,2,16,128]{3,2,1,0:T(8,128)S(1)} %get-tuple-element.19.fresh, f32[15,2,16,128]{3,2,1,0:T(8,128)S(1)} %get-tuple-element.20.mate, ...), custom_call_target="tpu_custom_call" | custom-call | tf_op jit(solution)/shard_map/pallas_call | solution.py:344
Async XLA Ops:
  0.0 1.1 %copy-start = (f32[1,10,8,16,128]{4,3,2,1,0:T(8,128)S(1)}, f32[1,10,8,16,128]{4,3,2,1,0:T(8,128)}, u32[]{:S(2)}) copy-start(f32[1,10,8,16,128]{4,3,2,1,0:T(8,128)} %state.1) | copy-start | bytes 1966084
  1.1 0.8 %copy-start.1 = (s32[1,8,16,128]{3,2,1,0:T(8,128)S(1)}, s32[1,8,16,128]{3,2,1,0:T(8,128)}, u32[]{:S(2)}) copy-start(s32[1,8,16,128]{3,2,1,0:T(8,128)} %damage.1) | copy-start | bytes 196612
  1.9 0.7 %copy-start.2 = (s32[16,128]{1,0:T(8,128)S(1)}, s32[16,128]{1,0:T(8,128)}, u32[]{:S(2)}) copy-start(s32[16,128]{1,0:T(8,128)} %frame.1) | copy-start | bytes 24580
  2.6 0.7 %copy-start.3 = (s32[16,128]{1,0:T(8,128)S(1)}, s32[16,128]{1,0:T(8,128)}, u32[]{:S(2)}) copy-start(s32[16,128]{1,0:T(8,128)} %impact.1) | copy-start | bytes 24580
  4.8 15.1 %collective-permute-start = (f32[6,16,128]{2,1,0:T(8,128)S(1)}, f32[6,16,128]{2,1,0:T(8,128)S(1)}, u32[]{:S(2)}, u32[]{:S(2)}) collective-permute-start(f32[6,16,128]{2,1,0:T(8,128)S(1)} %get-tuple-element.16), channel_id=1, source_target_pairs={{1,2},{2,1},{3,4},{4,3},{5,6},{6,5},{7,8},{8,7},{9,10},{10,9},{11,... | collective-permute-start | bytes 147464 | tf_op jit(solution)/shard_map/ppermute | solution.py:375

commit v4 on v3

--- a/solution.py
+++ b/solution.py
@@ -19,11 +19,14 @@
 
 VX, VY, VZ, SXX, SYY, SZZ, SXY, SXZ, SYZ, SCALE = range(10)
 DISP, KEEP, PUSH, OWN = 80, 81, 82, 83
-DISP_ALL = 83
+SPARE = 83
 MATE = 83
 ALL = 98
 M_VX, M_VY, M_VZ, M_W, M_XX, M_YY, M_XY, M_XZ, M_YZ = range(MATE, MATE + 9)
 M_XZ1, M_YZ1, M_ZZ1, M_XZ2, M_YZ2, M_ZZ2 = range(MATE + 9, MATE + 15)
+
+PICKS = [(VX, 0), (VY, 0), (VZ, 0), None, (SXX, 0), (SYY, 0), (SXY, 0), (SXZ, 0), (SYZ, 0)]
+PICKS += [(f, depth) for depth in (1, 2) for f in (SXZ, SYZ, SZZ)]
 
 PER_GROUP = 16
 GROUPS = 6
@@ -155,14 +158,14 @@
             put(at(f, z), fresh * keep)
 
 
-def fetch_kernel(state, damage, frame, impact, tile, near, far, levels, held, struck, arrived):
+def fetch_kernel(state, damage, frame, impact, near, far, surface, tile, levels, held, struck, arrived):
     copies = [
         pltpu.make_async_copy(damage.at[0], levels, arrived.at[10]),
         pltpu.make_async_copy(frame, held, arrived.at[11]),
         pltpu.make_async_copy(impact, struck, arrived.at[12]),
     ]
     for f in range(10):
-        first = DISP_ALL if f == 9 else at(f, 0)
+        first = SPARE if f == 9 else at(f, 0)
         copies.append(
             pltpu.make_async_copy(state.at[0, f], tile.at[pl.ds(first, THICK)], arrived.at[f])
         )
@@ -174,7 +177,7 @@
     even = lax.axis_index("hgt") % 2 == 0
     for z in range(THICK):
         tile[at(SCALE, z)] = 1.0 - softening * levels[z].astype(jnp.float32)
-    tile[DISP] = jnp.where(front, tile[DISP_ALL + THICK - 1], tile[DISP_ALL])
+    tile[DISP] = jnp.where(front, tile[SPARE + THICK - 1], tile[SPARE])
     tile[KEEP] = (1 - held[...]).astype(jnp.float32)
     tile[PUSH] = struck[...].astype(jnp.float32)
     slot = lanes_of(ROWS) // HALO
@@ -187,9 +190,15 @@
             last = jnp.where(slot == j, turn(plane, HALO * j + HALO), last)
         near[g] = jnp.where(even, last, first)
         far[g] = jnp.where(even, first, last)
-
-
-def side_kernel(tile, near, far, side, surface):
+    for k, pick in enumerate(PICKS):
+        if pick is None:
+            surface[k] = tile[DISP]
+        else:
+            low, high = at(pick[0], pick[1]), at(pick[0], THICK - 1 - pick[1])
+            surface[k] = jnp.where(front, tile[high], tile[low])
+
+
+def side_kernel(own, near, far, side, surface):
     front = lax.axis_index("ply") == 0
     place = lax.axis_index("hgt")
     even = place % 2 == 0
@@ -203,23 +212,27 @@
             r = turn(from_right, -HALO * j)
             m = turn(from_left, -HALO - HALO * j)
             side[g * PER_GROUP + j] = jnp.where(is_right, r, jnp.where(is_left, m, 0.0))
-    picks = [(VX, 0), (VY, 0), (VZ, 0), None, (SXX, 0), (SYY, 0), (SXY, 0), (SXZ, 0), (SYZ, 0)]
-    picks += [(f, depth) for depth in (1, 2) for f in (SXZ, SYZ, SZZ)]
     sides = []
-    for k, pick in enumerate(picks):
+    for k, pick in enumerate(PICKS):
+        surface[k] = own[k]
         if pick is None:
-            surface[k] = tile[DISP]
             sides.append(side[DISP])
         else:
             low, high = at(pick[0], pick[1]), at(pick[0], THICK - 1 - pick[1])
-            surface[k] = jnp.where(front, tile[high], tile[low])
             sides.append(jnp.where(front, side[high], side[low]))
     surface[15] = pack_sides(sides[:8])
     surface[16] = pack_sides(sides[8:])
 
 
-def speed_kernel(tile, side, mates, fresh, mate, near, far, middle, flank):
+def speed_kernel(
+    state, damage, frame, impact, side, mates, fresh, mate, extra, near, far, middle, flank
+):
     front = lax.axis_index("ply") == 0
+    for z in range(THICK):
+        extra[z] = 1.0 - softening * damage[0, z].astype(jnp.float32)
+    extra[DISP - 72] = jnp.where(front, state[0, 9, THICK - 1], state[0, 9, 0])
+    extra[KEEP - 72] = (1 - frame[...]).astype(jnp.float32)
+    extra[PUSH - 72] = impact[...].astype(jnp.float32)
     core = lax.axis_index("len") % 2
     other = jnp.where(front, 1, 0)
     for k in range(15):
@@ -229,7 +242,11 @@
     def look(plane, r, n):
         if plane >= MATE:
             return mate[plane - MATE, :, r : r + n, :]
-        return jnp.stack([tile[plane, r : r + n, :], side[plane, r : r + n, :]])
+        if plane >= 72:
+            main = extra[plane - 72, r : r + n, :]
+        else:
+            main = state[0, plane // THICK, plane % THICK, r : r + n, :]
+        return jnp.stack([main, side[plane, r : r + n, :]])
 
     def put(plane, value):
         fresh[plane if plane < 24 else 24 + plane - MATE, :, 2 : ROWS - 2, :] = value
@@ -251,7 +268,7 @@
             out[SENT + g] = pack_sides([flank[way, k] for k in ks])
 
 
-def last_kernel(tile, side, fresh, mate, near, far, out, cells):
+def last_kernel(state, extra, side, fresh, mate, near, far, out, cells):
     front = lax.axis_index("ply") == 0
     index = lax.axis_index("len")
     upper = index % 2 == 0
@@ -259,7 +276,11 @@
     has_bottom = index < lax.axis_size("len") - 1
 
     for plane in range(OWN):
-        cells[plane, 0, HALO : HALO + ROWS, :] = tile[plane]
+        if plane >= 72:
+            main = extra[plane - 72]
+        else:
+            main = state[0, plane // THICK, plane % THICK]
+        cells[plane, 0, HALO : HALO + ROWS, :] = main
         cells[plane, 1, HALO : HALO + ROWS, :] = side[plane]
     for k in range(15):
         cells[MATE + k, :, HALO : HALO + ROWS, :] = mate[k]
@@ -269,7 +290,7 @@
     for down, there in ((1, has_top), (0, has_bottom)):
 
         def sent(k):
-            first, second = (far[0, k], near[0, k]) if down else (near[1, k], far[1, k])
+            first, second = (far[k], near[0, k]) if down else (near[1, k], far[k])
             return jnp.where(there, jnp.where(upper, first, second), 0.0)
 
         packed = [sent(SENT + g) for g in range(SENT_SIDES)]
@@ -326,7 +347,7 @@
     for z in range(THICK):
         for f, change in enumerate(changes(z, r, n, 2)):
             put(at(SXX + f, z), look(at(SXX + f, z), r, n) + change)
-        out[0, 9, z] = tile[DISP_ALL + z] + time_step * look(at(VZ, z), 0, ROWS)[0]
+        out[0, 9, z] = state[0, 9, z] + time_step * look(at(VZ, z), 0, ROWS)[0]
     new_velocities(look, -2, ROWS + 4, front, writer(-2, ROWS + 4), False)
     for z in range(THICK):
         for f in range(3):
@@ -351,20 +372,21 @@
     )(*args)
 
 
-FETCH_LIMIT = 32 * MIB
+FETCH_LIMIT = 60 * MIB
 
 
 def per_device(plate_state, damage, frame_mask, impact_mask):
     even = [[2 * i, 2 * i + 1] for i in range(8)]
     odd = [[2 * i + 1, (2 * i + 2) % 16] for i in range(8)]
     strips = shaped(GROUPS, ROWS, LANES)
-    tile, near, far = call(
+    near, far, surface = call(
         fetch_kernel,
-        [shaped(OWN + THICK, ROWS, LANES), strips, strips],
+        [strips, strips, shaped(15, ROWS, LANES)],
         (plate_state, damage, frame_mask, impact_mask),
         limit=FETCH_LIMIT,
         space=pl.ANY,
         scratch=[
+            pltpu.VMEM((OWN + THICK, ROWS, LANES), jnp.float32),
             pltpu.VMEM((THICK, ROWS, LANES), jnp.int32),
             pltpu.VMEM((ROWS, LANES), jnp.int32),
             pltpu.VMEM((ROWS, LANES), jnp.int32),
@@ -377,22 +399,28 @@
     side, surface = call(
         side_kernel,
         [shaped(OWN, ROWS, LANES), shaped(MATE_SENT, ROWS, LANES)],
-        (tile, near, far),
+        (surface, near, far),
     )
     mates = lax.all_gather(surface, "ply")
     sent = shaped(SENT_ALL, HALO, LANES)
-    fresh, mate, near, far = call(
+    fresh, mate, extra, near, far = call(
         speed_kernel,
-        [shaped(27, 2, ROWS, LANES), shaped(15, 2, ROWS, LANES), sent, sent],
-        (tile, side, mates),
+        [
+            shaped(27, 2, ROWS, LANES),
+            shaped(15, 2, ROWS, LANES),
+            shaped(11, ROWS, LANES),
+            sent,
+            sent,
+        ],
+        (plate_state, damage, frame_mask, impact_mask, side, mates),
         scratch=[pltpu.VMEM((2, SENT, HALO, LANES), jnp.float32)] * 2,
     )
+    far = lax.ppermute(far, "len", swap)
     near = lax.all_gather(near, "len", axis_index_groups=even)
-    far = lax.all_gather(far, "len", axis_index_groups=odd)
     return call(
         last_kernel,
         shaped(1, 10, THICK, ROWS, LANES),
-        (tile, side, fresh, mate, near, far),
+        (plate_state, extra, side, fresh, mate, near, far),
         scratch=[pltpu.VMEM((ALL, 2, ROWS + 2 * HALO, LANES), jnp.float32)],
     )
 

time: 41.6 us -> 38.7 us (0.930)
  blocking collectives: 20.3 us -> 10.7 us
  starting transfers between devices: 11.5 us -> 19.2 us
  local copies, waits for them, and re-layouts: 3.32 us -> 0.03 us
  waiting for transfers between devices: 0.01 us -> 1.41 us
  Pallas kernels: 6.13 us -> 7.1 us
    ppermute x0 -> x1, starting transfers between devices: none -> 7.56 us  [per_device(): far = lax.ppermute(far, 'len', swap)]
    all_gather x1 -> x0, blocking collectives: 7.15 us -> none  [per_device(): far = lax.all_gather(far, 'len', axis_index_groups=odd)]
    unnamed x8 -> x10, local copies, waits for them, and re-layouts: 3.32 us -> 0.03 us
    all_gather x1, blocking collectives: 4.99 us -> 2.11 us  [per_device(): near = lax.all_gather(near, 'len', axis_index_groups=even)]
    ppermute x0 -> x1, waiting for transfers between devices: none -> 1.4 us  [per_device(): far = lax.ppermute(far, 'len', swap)]
    pallas_call x4, Pallas kernels: 6.13 us -> 7.1 us  [call(): pl.pallas_call(kernel, out_shape=outs, in_specs=[pl.BlockSpec(memory_spac...]
  transfers between devices with their start and end apart: 1 -> 2, of which waited for: 0 -> 1; matrix products, arithmetic and copies ran while one was open for 0% -> 0% of each run, Pallas kernels for 0% -> 0%
where the time goes in v4:
time: 38.7 us; the launch traced here: 38.5 us
  starting transfers between devices  19.2 us (50%)
  blocking collectives  10.7 us (28%)
  Pallas kernels  7.1 us (18%)
  waiting for transfers between devices  1.41 us (4%)
    ppermute x1, starting transfers between devices, per_device(): far = lax.ppermute(far, 'hgt', swap)  11.6 us
    ppermute x1, starting transfers between devices, per_device(): far = lax.ppermute(far, 'len', swap)  7.56 us
    pallas_call x4, Pallas kernels, call(): pl.pallas_call(kernel, out_shape=outs, in_specs=[pl.BlockSpec(memory_spac...  7.1 us
    all_gather x1, blocking collectives, per_device(): mates = lax.all_gather(surface, 'ply')  4.71 us
    all_gather x1, blocking collectives, per_device(): near = lax.all_gather(near, 'hgt', axis_index_groups=even)  3.83 us
    all_gather x1, blocking collectives, per_device(): near = lax.all_gather(near, 'len', axis_index_groups=even)  2.11 us
    ppermute x1, waiting for transfers between devices, per_device(): far = lax.ppermute(far, 'len', swap)  1.4 us
  transfers between devices with their start and end apart: 2, of which 1 were waited for; matrix products, arithmetic and copies ran while one was open for 0% of the time, Pallas kernels for 0%

profile of v4, /device:TPU:31, one launch (start us, length us, event | category | flops | bytes accessed | tf_op | source)
XLA Modules:
  0.0 38.5 jit_solution(1326271029630251846)
XLA Ops:
  0.0 0.0 copy-start
  0.0 2.4 %shard_map.46 = (f32[6,16,128]{2,1,0:T(8,128)}, f32[6,16,128]{2,1,0:T(8,128)}, f32[15,16,128]{2,1,0:T(8,128)}) custom-call(f32[1,10,8,16,128]{4,3,2,1,0:T(8,128)} %state.5, s32[1,8,16,128]{3,2,1,0:T(8,128)} %damage.3, s32[16,128]{1,0:T(8,128)} %frame.3, s32[16,128]{1,0:T(8,128)} %impact.3), custom_call_target="tpu_custom_call" | custom-call | tf_op jit(solution)/shard_map/pallas_call | solution.py:365
  2.4 0.0 copy-start.2
  2.4 11.6 %collective-permute-start = (f32[6,16,128]{2,1,0:T(8,128)}, f32[6,16,128]{2,1,0:T(8,128)S(1)}, u32[]{:S(2)}, u32[]{:S(2)}) collective-permute-start(f32[6,16,128]{2,1,0:T(8,128)} %get-tuple-element.17), channel_id=1, source_target_pairs={{1,2},{2,1},{3,4},{4,3},{5,6},{6,5},{7,8},{8,7},{9,10},{10,9},{11,... | collective-permute-start | bytes 147464 | tf_op jit(solution)/shard_map/ppermute | solution.py:397
  14.1 3.8 %all-gather = f32[12,16,128]{2,1,0:T(8,128)S(1)} all-gather(f32[6,16,128]{2,1,0:T(8,128)} %get-tuple-element.16), channel_id=2, replica_groups={{0,1},{2,3},{4,5},{6,7},{8,9},{10,11},{12,13},{14,15},{16,17},{18,19},{..., dimensions={0}, use_global_device_ids=true | all-gather | bytes 147456 | tf_op jit(solution)/shard_map/all_gather | solution.py:398
  17.9 0.0 collective-permute-done.far
  17.9 0.0 copy-done.2
  17.9 0.5 %shard_map.47 = (f32[83,16,128]{2,1,0:T(8,128)S(1)}, f32[17,16,128]{2,1,0:T(8,128)S(1)}) custom-call(f32[15,16,128]{2,1,0:T(8,128)S(1)} %copy-done.2, f32[2,6,16,128]{3,2,1,0:T(8,128)S(1)} %bitcast.5, f32[6,16,128]{2,1,0:T(8,128)S(1)} %collective-permute-done.far), custom_call_target="tpu_custom_call" | custom-call | tf_op jit(solution)/shard_map/pallas_call | solution.py:365
  18.4 0.0 copy-start.1
  18.4 0.0 copy-start.3
  18.4 0.0 copy-start.4
  18.4 4.7 %all-gather.1 = f32[34,16,128]{2,1,0:T(8,128)S(1)} all-gather(f32[17,16,128]{2,1,0:T(8,128)S(1)} %get-tuple-element.19), channel_id=3, replica_groups=mesh['ply'=2,'len'=16,'hgt'=16] {'ply'}, dimensions={0}, use_global_device_ids=true | all-gather | bytes 417792 | tf_op jit(solution)/shard_map/all_gather | solution.py:404
  23.1 0.0 copy-done
  23.1 0.0 copy-done.1
  23.1 0.0 copy-done.3
  23.2 0.0 copy-done.4
  23.2 0.9 %shard_map.48 = (f32[27,2,16,128]{3,2,1,0:T(8,128)S(1)}, f32[15,2,16,128]{3,2,1,0:T(8,128)S(1)}, f32[11,16,128]{2,1,0:T(8,128)S(1)}, f32[52,8,128]{2,1,0:T(8,128)S(1)}, f32[52,8,128]{2,1,0:T(8,128)S(1)}) custom-call(f32[1,10,8,16,128]{4,3,2,1,0:T(8,128)S(1)} %copy-done, s32[1,8,16,128]{3,2,1,0:T(8,128)S(1)} %copy-done.1, s32[16,128]{1,0:T(8,128)S(1)} %copy-done.3, ...), custom_call_target="tpu_custom_call" | custom-call | tf_op jit(solution)/shard_map/pallas_call | solution.py:365
  24.1 7.6 %collective-permute-start.1 = (f32[52,8,128]{2,1,0:T(8,128)S(1)}, f32[52,8,128]{2,1,0:T(8,128)S(1)}, u32[]{:S(2)}, u32[]{:S(2)}) collective-permute-start(f32[52,8,128]{2,1,0:T(8,128)S(1)} %get-tuple-element.24), channel_id=1, source_target_pairs={{16,32},{32,16},{48,64},{64,48},{80,96},{96,80},{112,128},{128,112... | collective-permute-start | bytes 638984 | tf_op jit(solution)/shard_map/ppermute | solution.py:418
  31.6 2.1 %all-gather.2 = f32[104,8,128]{2,1,0:T(8,128)S(1)} all-gather(f32[52,8,128]{2,1,0:T(8,128)S(1)} %get-tuple-element.23), channel_id=4, replica_groups={{0,16},{32,48},{64,80},{96,112},{128,144},{160,176},{192,208},{224,240}..., dimensions={0}, use_global_device_ids=true | all-gather | bytes 638976 | tf_op jit(solution)/shard_map/all_gather | solution.py:419
  33.7 1.4 %collective-permute-done.1.far = f32[52,8,128]{2,1,0:T(8,128)S(1)} collective-permute-done((f32[52,8,128]{2,1,0:T(8,128)S(1)}, f32[52,8,128]{2,1,0:T(8,128)S(1)}, u32[]{:S(2)}, u32[]{:S(2)}) %collective-permute-start.1) | collective-permute-done | bytes 213024 | tf_op jit(solution)/shard_map/ppermute | solution.py:418
  35.1 3.3 %shard_map.49 = f32[1,10,8,16,128]{4,3,2,1,0:T(8,128)} custom-call(f32[1,10,8,16,128]{4,3,2,1,0:T(8,128)S(1)} %copy-done, f32[11,16,128]{2,1,0:T(8,128)S(1)} %get-tuple-element.20.extra, f32[83,16,128]{2,1,0:T(8,128)S(1)} %get-tuple-element.18.side, f32[27,2,16,128]{3,2,1,0:T(8,128)S(1)} %get-tuple-element.21.fresh, ...), custom_call_target="tpu_custom_call" | custom-call | tf_op jit(solution)/shard_map/pallas_call | solution.py:365
Async XLA Ops:
  0.0 23.1 %copy-start = (f32[1,10,8,16,128]{4,3,2,1,0:T(8,128)S(1)}, f32[1,10,8,16,128]{4,3,2,1,0:T(8,128)}, u32[]{:S(2)}) copy-start(f32[1,10,8,16,128]{4,3,2,1,0:T(8,128)} %state.5) | copy-start | bytes 1966084
  2.4 15.5 %copy-start.2 = (f32[15,16,128]{2,1,0:T(8,128)S(1)}, f32[15,16,128]{2,1,0:T(8,128)}, u32[]{:S(2)}) copy-start(f32[15,16,128]{2,1,0:T(8,128)} %get-tuple-element.15.own) | copy-start | bytes 368644
  2.4 15.5 %collective-permute-start = (f32[6,16,128]{2,1,0:T(8,128)}, f32[6,16,128]{2,1,0:T(8,128)S(1)}, u32[]{:S(2)}, u32[]{:S(2)}) collective-permute-start(f32[6,16,128]{2,1,0:T(8,128)} %get-tuple-element.17), channel_id=1, source_target_pairs={{1,2},{2,1},{3,4},{4,3},{5,6},{6,5},{7,8},{8,7},{9,10},{10,9},{11,... | collective-permute-start | bytes 147464 | tf_op jit(solution)/shard_map/ppermute | solution.py:397
  18.4 4.8 %copy-start.1 = (s32[1,8,16,128]{3,2,1,0:T(8,128)S(1)}, s32[1,8,16,128]{3,2,1,0:T(8,128)}, u32[]{:S(2)}) copy-start(s32[1,8,16,128]{3,2,1,0:T(8,128)} %damage.3) | copy-start | bytes 196612
  18.4 4.7 %copy-start.3 = (s32[16,128]{1,0:T(8,128)S(1)}, s32[16,128]{1,0:T(8,128)}, u32[]{:S(2)}) copy-start(s32[16,128]{1,0:T(8,128)} %frame.3) | copy-start | bytes 24580
  18.4 4.7 %copy-start.4 = (s32[16,128]{1,0:T(8,128)S(1)}, s32[16,128]{1,0:T(8,128)}, u32[]{:S(2)}) copy-start(s32[16,128]{1,0:T(8,128)} %impact.3) | copy-start | bytes 24580
  24.1 11.1 %collective-permute-start.1 = (f32[52,8,128]{2,1,0:T(8,128)S(1)}, f32[52,8,128]{2,1,0:T(8,128)S(1)}, u32[]{:S(2)}, u32[]{:S(2)}) collective-permute-start(f32[52,8,128]{2,1,0:T(8,128)S(1)} %get-tuple-element.24), channel_id=1, source_target_pairs={{16,32},{32,16},{48,64},{64,48},{80,96},{96,80},{112,128},{128,112... | collective-permute-start | bytes 638984 | tf_op jit(solution)/shard_map/ppermute | solution.py:418

commit v5 on v4

--- a/solution.py
+++ b/solution.py
@@ -21,16 +21,16 @@
 DISP, KEEP, PUSH, OWN = 80, 81, 82, 83
 SPARE = 83
 MATE = 83
-ALL = 98
-M_VX, M_VY, M_VZ, M_W, M_XX, M_YY, M_XY, M_XZ, M_YZ = range(MATE, MATE + 9)
-M_XZ1, M_YZ1, M_ZZ1, M_XZ2, M_YZ2, M_ZZ2 = range(MATE + 9, MATE + 15)
+MATES = 10
+ALL = MATE + MATES
+M_VX, M_VY, M_VZ, M_W, M_XX, M_XY, M_XZ, M_FX, M_FY, M_FZ = range(MATE, ALL)
 
 PICKS = [(VX, 0), (VY, 0), (VZ, 0), None, (SXX, 0), (SYY, 0), (SXY, 0), (SXZ, 0), (SYZ, 0)]
 PICKS += [(f, depth) for depth in (1, 2) for f in (SXZ, SYZ, SZZ)]
 
 PER_GROUP = 16
 GROUPS = 6
-MATE_SENT = 17
+MATE_SENT = MATES + 2
 
 VMEM = pl.BlockSpec(memory_space=pltpu.VMEM)
 MIB = 2**20
@@ -48,7 +48,7 @@
 
 def twos():
     items = [at(f, z) for f in (SYY, SZZ, SYZ, VX, VY, VZ) for z in range(THICK)]
-    items += [M_VX, M_VY, M_VZ, M_W, M_YY, M_YZ, M_XZ1, M_YZ1, M_ZZ1, M_XZ2, M_YZ2, M_ZZ2]
+    items += [M_VX, M_VY, M_VZ, M_W, M_FX, M_FY, M_FZ]
     return items + [DISP, KEEP, PUSH]
 
 
@@ -132,14 +132,8 @@
     pull = [time_step * p for p in pull]
     push = jnp.where(front, time_step * pressure, 0.0) * look(PUSH, r0, n)
     if with_mate:
-        sign = jnp.where(front, 1.0, -1.0)
-        parts = ((M_XX, M_XY, M_XZ1, M_XZ2), (M_XY, M_YY, M_YZ1, M_YZ2), (M_XZ, M_YZ, M_ZZ1, M_ZZ2))
-        for f, (a, b, one, two) in enumerate(parts):
-            total = (
-                along_length(look, a, r0, n)
-                + along_height(look(b, r0, n))
-                + sign * (8.0 * look(one, r0, n) - look(two, r0, n))
-            )
+        for f, (a, force) in enumerate(((M_XX, M_FX), (M_XY, M_FY), (M_XZ, M_FZ))):
+            total = along_length(look, a, r0, n) + look(force, r0, n)
             put(M_VX + f, (mate[f] + STEP * total - pull[f]) * keep)
     for z in range(THICK):
         for f, (a, b, c) in enumerate(((SXX, SXY, SXZ), (SXY, SYY, SYZ), (SXZ, SYZ, SZZ))):
@@ -158,7 +152,7 @@
             put(at(f, z), fresh * keep)
 
 
-def fetch_kernel(state, damage, frame, impact, near, far, surface, tile, levels, held, struck, arrived):
+def fetch_kernel(state, damage, frame, impact, near, far, again, tile, levels, held, struck, arrived):
     copies = [
         pltpu.make_async_copy(damage.at[0], levels, arrived.at[10]),
         pltpu.make_async_copy(frame, held, arrived.at[11]),
@@ -171,7 +165,7 @@
         )
     for copy in copies:
         copy.start()
-    for copy in copies:
+    for copy in (*copies[:3], copies[12]):
         copy.wait()
     front = lax.axis_index("ply") == 0
     even = lax.axis_index("hgt") % 2 == 0
@@ -182,23 +176,19 @@
     tile[PUSH] = struck[...].astype(jnp.float32)
     slot = lanes_of(ROWS) // HALO
     for g in range(GROUPS):
+        for copy in copies[3 + 2 * g : min(5 + 2 * g, 12)]:
+            copy.wait()
         first = jnp.zeros((ROWS, LANES), jnp.float32)
         last = first
         for j in range(min(PER_GROUP, OWN - g * PER_GROUP)):
             plane = tile[g * PER_GROUP + j]
             first = jnp.where(slot == j, turn(plane, HALO * j), first)
             last = jnp.where(slot == j, turn(plane, HALO * j + HALO), last)
-        near[g] = jnp.where(even, last, first)
+        near[g] = again[g] = jnp.where(even, last, first)
         far[g] = jnp.where(even, first, last)
-    for k, pick in enumerate(PICKS):
-        if pick is None:
-            surface[k] = tile[DISP]
-        else:
-            low, high = at(pick[0], pick[1]), at(pick[0], THICK - 1 - pick[1])
-            surface[k] = jnp.where(front, tile[high], tile[low])
-
-
-def side_kernel(own, near, far, side, surface):
+
+
+def side_kernel(state, high, far, low, side, surface):
     front = lax.axis_index("ply") == 0
     place = lax.axis_index("hgt")
     even = place % 2 == 0
@@ -206,22 +196,32 @@
     is_right = (lane < HALO) & (place < lax.axis_size("hgt") - 1)
     is_left = (lane >= LANES - HALO) & (place > 0)
     for g in range(GROUPS):
-        from_right = jnp.where(even, near[1, g], far[g])
-        from_left = jnp.where(even, far[g], near[0, g])
+        near = jnp.where(place < lax.axis_size("hgt") // 2, low[g], high[g])
+        from_right = jnp.where(even, near, far[g])
+        from_left = jnp.where(even, far[g], near)
         for j in range(min(PER_GROUP, OWN - g * PER_GROUP)):
             r = turn(from_right, -HALO * j)
             m = turn(from_left, -HALO - HALO * j)
             side[g * PER_GROUP + j] = jnp.where(is_right, r, jnp.where(is_left, m, 0.0))
-    sides = []
+    full = []
     for k, pick in enumerate(PICKS):
-        surface[k] = own[k]
         if pick is None:
-            sides.append(side[DISP])
+            main = jnp.where(front, state[0, 9, THICK - 1], state[0, 9, 0])
+            flank = side[DISP]
         else:
-            low, high = at(pick[0], pick[1]), at(pick[0], THICK - 1 - pick[1])
-            sides.append(jnp.where(front, side[high], side[low]))
-    surface[15] = pack_sides(sides[:8])
-    surface[16] = pack_sides(sides[8:])
+            f, less, more = pick[0], pick[1], THICK - 1 - pick[1]
+            main = jnp.where(front, state[0, f, more], state[0, f, less])
+            flank = jnp.where(front, side[at(f, more)], side[at(f, less)])
+        full.append(jnp.stack([main, flank]))
+    up = jnp.where(front, -1.0, 1.0)
+    sent = full[:5] + full[6:8]
+    for crossing, one, two in ((6, 9, 12), (5, 10, 13), (8, 11, 14)):
+        sent.append(along_height(full[crossing]) + up * (8.0 * full[one] - full[two]))
+    for k, planes in enumerate(sent):
+        surface[k] = planes[0]
+    flanks = [planes[1] for planes in sent]
+    surface[MATES] = pack_sides(flanks[:8])
+    surface[MATES + 1] = pack_sides(flanks[8:])
 
 
 def speed_kernel(
@@ -235,9 +235,9 @@
     extra[PUSH - 72] = impact[...].astype(jnp.float32)
     core = lax.axis_index("len") % 2
     other = jnp.where(front, 1, 0)
-    for k in range(15):
+    for k in range(MATES):
         mate[k, 0] = mates[other, k]
-        mate[k, 1] = unpack_side(mates[other, 15 + k // 8], k % 8)
+        mate[k, 1] = unpack_side(mates[other, MATES + k // 8], k % 8)
 
     def look(plane, r, n):
         if plane >= MATE:
@@ -282,7 +282,7 @@
             main = state[0, plane // THICK, plane % THICK]
         cells[plane, 0, HALO : HALO + ROWS, :] = main
         cells[plane, 1, HALO : HALO + ROWS, :] = side[plane]
-    for k in range(15):
+    for k in range(MATES):
         cells[MATE + k, :, HALO : HALO + ROWS, :] = mate[k]
     for k in range(27):
         plane = k if k < 24 else MATE + k - 24
@@ -379,9 +379,9 @@
     even = [[2 * i, 2 * i + 1] for i in range(8)]
     odd = [[2 * i + 1, (2 * i + 2) % 16] for i in range(8)]
     strips = shaped(GROUPS, ROWS, LANES)
-    near, far, surface = call(
+    near, far, again = call(
         fetch_kernel,
-        [strips, strips, shaped(15, ROWS, LANES)],
+        [strips, strips, strips],
         (plate_state, damage, frame_mask, impact_mask),
         limit=FETCH_LIMIT,
         space=pl.ANY,
@@ -394,12 +394,14 @@
         ],
     )
     swap = [(i, j) for pair in odd[:-1] for i, j in (pair, pair[::-1])]
+    both = lambda pairs: [(i, j) for pair in pairs for i, j in (pair, pair[::-1])]
+    high = lax.ppermute(near, "hgt", both(even[4:]))
     far = lax.ppermute(far, "hgt", swap)
-    near = lax.all_gather(near, "hgt", axis_index_groups=even)
+    low = lax.ppermute(again, "hgt", both(even[:4]))
     side, surface = call(
         side_kernel,
         [shaped(OWN, ROWS, LANES), shaped(MATE_SENT, ROWS, LANES)],
-        (surface, near, far),
+        (plate_state, high, far, low),
     )
     mates = lax.all_gather(surface, "ply")
     sent = shaped(SENT_ALL, HALO, LANES)
@@ -407,7 +409,7 @@
         speed_kernel,
         [
             shaped(27, 2, ROWS, LANES),
-            shaped(15, 2, ROWS, LANES),
+            shaped(MATES, 2, ROWS, LANES),
             shaped(11, ROWS, LANES),
             sent,
             sent,

time: 38.7 us -> 36.2 us (0.935)
  blocking collectives: 10.7 us -> 6.37 us
  waiting for transfers between devices: 1.41 us -> 2.32 us
  starting transfers between devices: 19.2 us -> 19.9 us
    ppermute x0 -> x2, starting transfers between devices: none -> 4.66 us  [the longest x1 4 us: per_device(): high = lax.ppermute(near, 'hgt', both(even[4:]))]
    all_gather x1 -> x0, blocking collectives: 3.83 us -> none  [per_device(): near = lax.all_gather(near, 'hgt', axis_index_groups=even)]
    ppermute x1, starting transfers between devices: 11.6 us -> 8.17 us  [per_device(): far = lax.ppermute(far, 'hgt', swap)]
    ppermute x1, waiting for transfers between devices: 0.01 us -> 0.99 us  [per_device(): far = lax.ppermute(far, 'hgt', swap)]
    ppermute x1, starting transfers between devices: 7.56 us -> 7.1 us  [per_device(): far = lax.ppermute(far, 'len', swap)]
    all_gather x1, blocking collectives: 4.71 us -> 4.27 us  [per_device(): mates = lax.all_gather(surface, 'ply')]
  transfers between devices with their start and end apart: 2 -> 4, of which waited for: 1 -> 2; matrix products, arithmetic and copies ran while one was open for 0% -> 0% of each run, Pallas kernels for 0% -> 0%
where the time goes in v5:
time: 36.2 us; the launch traced here: 36 us
  starting transfers between devices  19.9 us (55%)
  Pallas kernels  7.3 us (20%)
  blocking collectives  6.37 us (18%)
  waiting for transfers between devices  2.32 us (6%)
    ppermute x1, starting transfers between devices, per_device(): far = lax.ppermute(far, 'hgt', swap)  8.17 us
    pallas_call x4, Pallas kernels, call(): pl.pallas_call(kernel, out_shape=outs, in_specs=[pl.BlockSpec(memory_spac...  7.3 us
    ppermute x1, starting transfers between devices, per_device(): far = lax.ppermute(far, 'len', swap)  7.1 us
    all_gather x1, blocking collectives, per_device(): mates = lax.all_gather(surface, 'ply')  4.27 us
    ppermute x1, starting transfers between devices, per_device(): high = lax.ppermute(near, 'hgt', both(even[4:]))  4 us
    all_gather x1, blocking collectives, per_device(): near = lax.all_gather(near, 'len', axis_index_groups=even)  2.1 us
    ppermute x1, waiting for transfers between devices, per_device(): far = lax.ppermute(far, 'len', swap)  1.33 us
    ppermute x1, waiting for transfers between devices, per_device(): far = lax.ppermute(far, 'hgt', swap)  0.99 us
  transfers between devices with their start and end apart: 4, of which 2 were waited for; matrix products, arithmetic and copies ran while one was open for 0% of the time, Pallas kernels for 0%

profile of v5, /device:TPU:31, one launch (start us, length us, event | category | flops | bytes accessed | tf_op | source)
XLA Modules:
  0.0 36.0 jit_solution(782064223481625569)
XLA Ops:
  0.0 0.0 copy-start
  0.0 2.7 %shard_map.46 = (f32[6,16,128]{2,1,0:T(8,128)}, f32[6,16,128]{2,1,0:T(8,128)}, f32[6,16,128]{2,1,0:T(8,128)}) custom-call(f32[1,10,8,16,128]{4,3,2,1,0:T(8,128)} %state.7, s32[1,8,16,128]{3,2,1,0:T(8,128)} %damage.3, s32[16,128]{1,0:T(8,128)} %frame.3, s32[16,128]{1,0:T(8,128)} %impact.3), custom_call_target="tpu_custom_call" | custom-call | tf_op jit(solution)/shard_map/pallas_call | solution.py:365
  2.7 4.0 %collective-permute-start = (f32[6,16,128]{2,1,0:T(8,128)}, f32[6,16,128]{2,1,0:T(8,128)S(1)}, u32[]{:S(2)}, u32[]{:S(2)}) collective-permute-start(f32[6,16,128]{2,1,0:T(8,128)} %get-tuple-element.15), channel_id=1, source_target_pairs={{8,9},{9,8},{10,11},{11,10},{12,13},{13,12},{14,15},{15,14},{24,25... | collective-permute-start | bytes 147464 | tf_op jit(solution)/shard_map/ppermute | solution.py:398
  6.7 8.2 %collective-permute-start.1 = (f32[6,16,128]{2,1,0:T(8,128)}, f32[6,16,128]{2,1,0:T(8,128)S(1)}, u32[]{:S(2)}, u32[]{:S(2)}) collective-permute-start(f32[6,16,128]{2,1,0:T(8,128)} %get-tuple-element.16), channel_id=1, source_target_pairs={{1,2},{2,1},{3,4},{4,3},{5,6},{6,5},{7,8},{8,7},{9,10},{10,9},{11,... | collective-permute-start | bytes 147464 | tf_op jit(solution)/shard_map/ppermute | solution.py:399
  14.9 0.7 %collective-permute-start.2 = (f32[6,16,128]{2,1,0:T(8,128)}, f32[6,16,128]{2,1,0:T(8,128)S(1)}, u32[]{:S(2)}, u32[]{:S(2)}) collective-permute-start(f32[6,16,128]{2,1,0:T(8,128)} %get-tuple-element.17), channel_id=1, source_target_pairs={{0,1},{1,0},{2,3},{3,2},{4,5},{5,4},{6,7},{7,6},{16,17},{17,16},{1... | collective-permute-start | bytes 147464 | tf_op jit(solution)/shard_map/ppermute | solution.py:400
  15.6 0.0 collective-permute-done.high
  15.6 1.0 %collective-permute-done.1.far = f32[6,16,128]{2,1,0:T(8,128)S(1)} collective-permute-done((f32[6,16,128]{2,1,0:T(8,128)}, f32[6,16,128]{2,1,0:T(8,128)S(1)}, u32[]{:S(2)}, u32[]{:S(2)}) %collective-permute-start.1) | collective-permute-done | bytes 49184 | tf_op jit(solution)/shard_map/ppermute | solution.py:399
  16.6 0.0 collective-permute-done.2.low
  16.6 0.0 copy-done
  16.6 0.5 %shard_map.47 = (f32[83,16,128]{2,1,0:T(8,128)S(1)}, f32[12,16,128]{2,1,0:T(8,128)S(1)}) custom-call(f32[1,10,8,16,128]{4,3,2,1,0:T(8,128)S(1)} %copy-done, f32[6,16,128]{2,1,0:T(8,128)S(1)} %collective-permute-done.high, f32[6,16,128]{2,1,0:T(8,128)S(1)} %collective-permute-done.1.far, f32[6,16,128]{2,1,0:T(8,128)S(1)} %collective-permute-done.2.low), custom_call_target="tpu_custom_call" | custom-call | tf_op jit(solution)/shard_map/pallas_call | solution.py:365
  17.1 0.0 copy-start.1
  17.1 0.0 copy-start.2
  17.1 0.0 copy-start.3
  17.1 4.3 %all-gather = f32[24,16,128]{2,1,0:T(8,128)S(1)} all-gather(f32[12,16,128]{2,1,0:T(8,128)S(1)} %get-tuple-element.19), channel_id=2, replica_groups=mesh['ply'=2,'len'=16,'hgt'=16] {'ply'}, dimensions={0}, use_global_device_ids=true | all-gather | bytes 294912 | tf_op jit(solution)/shard_map/all_gather | solution.py:406
  21.4 0.0 copy-done.1
  21.4 0.0 copy-done.2
  21.4 0.0 copy-done.3
  21.4 0.8 %shard_map.48 = (f32[27,2,16,128]{3,2,1,0:T(8,128)S(1)}, f32[10,2,16,128]{3,2,1,0:T(8,128)S(1)}, f32[11,16,128]{2,1,0:T(8,128)S(1)}, f32[50,8,128]{2,1,0:T(8,128)S(1)}, f32[50,8,128]{2,1,0:T(8,128)S(1)}) custom-call(f32[1,10,8,16,128]{4,3,2,1,0:T(8,128)S(1)} %copy-done, s32[1,8,16,128]{3,2,1,0:T(8,128)S(1)} %copy-done.1, s32[16,128]{1,0:T(8,128)S(1)} %copy-done.2, ...), custom_call_target="tpu_custom_call" | custom-call | tf_op jit(solution)/shard_map/pallas_call | solution.py:365
  22.2 7.1 %collective-permute-start.3 = (f32[50,8,128]{2,1,0:T(8,128)S(1)}, f32[50,8,128]{2,1,0:T(8,128)S(1)}, u32[]{:S(2)}, u32[]{:S(2)}) collective-permute-start(f32[50,8,128]{2,1,0:T(8,128)S(1)} %get-tuple-element.24), channel_id=1, source_target_pairs={{16,32},{32,16},{48,64},{64,48},{80,96},{96,80},{112,128},{128,112... | collective-permute-start | bytes 614408 | tf_op jit(solution)/shard_map/ppermute | solution.py:420
  29.3 2.1 %all-gather.1 = f32[100,8,128]{2,1,0:T(8,128)S(1)} all-gather(f32[50,8,128]{2,1,0:T(8,128)S(1)} %get-tuple-element.23), channel_id=3, replica_groups={{0,16},{32,48},{64,80},{96,112},{128,144},{160,176},{192,208},{224,240}..., dimensions={0}, use_global_device_ids=true | all-gather | bytes 614400 | tf_op jit(solution)/shard_map/all_gather | solution.py:421
  31.4 1.3 %collective-permute-done.3.far = f32[50,8,128]{2,1,0:T(8,128)S(1)} collective-permute-done((f32[50,8,128]{2,1,0:T(8,128)S(1)}, f32[50,8,128]{2,1,0:T(8,128)S(1)}, u32[]{:S(2)}, u32[]{:S(2)}) %collective-permute-start.3) | collective-permute-done | bytes 204832 | tf_op jit(solution)/shard_map/ppermute | solution.py:420
  32.7 3.3 %shard_map.49 = f32[1,10,8,16,128]{4,3,2,1,0:T(8,128)} custom-call(f32[1,10,8,16,128]{4,3,2,1,0:T(8,128)S(1)} %copy-done, f32[11,16,128]{2,1,0:T(8,128)S(1)} %get-tuple-element.20.extra, f32[83,16,128]{2,1,0:T(8,128)S(1)} %get-tuple-element.18.side, f32[27,2,16,128]{3,2,1,0:T(8,128)S(1)} %get-tuple-element.21.fresh, ...), custom_call_target="tpu_custom_call" | custom-call | tf_op jit(solution)/shard_map/pallas_call | solution.py:365
Async XLA Ops:
  0.0 16.6 %copy-start = (f32[1,10,8,16,128]{4,3,2,1,0:T(8,128)S(1)}, f32[1,10,8,16,128]{4,3,2,1,0:T(8,128)}, u32[]{:S(2)}) copy-start(f32[1,10,8,16,128]{4,3,2,1,0:T(8,128)} %state.7) | copy-start | bytes 1966084
  2.7 12.9 %collective-permute-start = (f32[6,16,128]{2,1,0:T(8,128)}, f32[6,16,128]{2,1,0:T(8,128)S(1)}, u32[]{:S(2)}, u32[]{:S(2)}) collective-permute-start(f32[6,16,128]{2,1,0:T(8,128)} %get-tuple-element.15), channel_id=1, source_target_pairs={{8,9},{9,8},{10,11},{11,10},{12,13},{13,12},{14,15},{15,14},{24,25... | collective-permute-start | bytes 147464 | tf_op jit(solution)/shard_map/ppermute | solution.py:398
  6.7 9.9 %collective-permute-start.1 = (f32[6,16,128]{2,1,0:T(8,128)}, f32[6,16,128]{2,1,0:T(8,128)S(1)}, u32[]{:S(2)}, u32[]{:S(2)}) collective-permute-start(f32[6,16,128]{2,1,0:T(8,128)} %get-tuple-element.16), channel_id=1, source_target_pairs={{1,2},{2,1},{3,4},{4,3},{5,6},{6,5},{7,8},{8,7},{9,10},{10,9},{11,... | collective-permute-start | bytes 147464 | tf_op jit(solution)/shard_map/ppermute | solution.py:399
  14.9 1.7 %collective-permute-start.2 = (f32[6,16,128]{2,1,0:T(8,128)}, f32[6,16,128]{2,1,0:T(8,128)S(1)}, u32[]{:S(2)}, u32[]{:S(2)}) collective-permute-start(f32[6,16,128]{2,1,0:T(8,128)} %get-tuple-element.17), channel_id=1, source_target_pairs={{0,1},{1,0},{2,3},{3,2},{4,5},{5,4},{6,7},{7,6},{16,17},{17,16},{1... | collective-permute-start | bytes 147464 | tf_op jit(solution)/shard_map/ppermute | solution.py:400
  17.1 4.3 %copy-start.1 = (s32[1,8,16,128]{3,2,1,0:T(8,128)S(1)}, s32[1,8,16,128]{3,2,1,0:T(8,128)}, u32[]{:S(2)}) copy-start(s32[1,8,16,128]{3,2,1,0:T(8,128)} %damage.3) | copy-start | bytes 196612
  17.1 4.3 %copy-start.2 = (s32[16,128]{1,0:T(8,128)S(1)}, s32[16,128]{1,0:T(8,128)}, u32[]{:S(2)}) copy-start(s32[16,128]{1,0:T(8,128)} %frame.3) | copy-start | bytes 24580
  17.1 4.3 %copy-start.3 = (s32[16,128]{1,0:T(8,128)S(1)}, s32[16,128]{1,0:T(8,128)}, u32[]{:S(2)}) copy-start(s32[16,128]{1,0:T(8,128)} %impact.3) | copy-start | bytes 24580
  22.2 10.5 %collective-permute-start.3 = (f32[50,8,128]{2,1,0:T(8,128)S(1)}, f32[50,8,128]{2,1,0:T(8,128)S(1)}, u32[]{:S(2)}, u32[]{:S(2)}) collective-permute-start(f32[50,8,128]{2,1,0:T(8,128)S(1)} %get-tuple-element.24), channel_id=1, source_target_pairs={{16,32},{32,16},{48,64},{64,48},{80,96},{96,80},{112,128},{128,112... | collective-permute-start | bytes 614408 | tf_op jit(solution)/shard_map/ppermute | solution.py:420

commit v6 on v5

--- a/solution.py
+++ b/solution.py
@@ -18,8 +18,8 @@
 STEP = time_step / 12.0
 
 VX, VY, VZ, SXX, SYY, SZZ, SXY, SXZ, SYZ, SCALE = range(10)
-DISP, KEEP, PUSH, OWN = 80, 81, 82, 83
-SPARE = 83
+SCALES, DISP, KEEP, PUSH, OWN = 72, 80, 81, 82, 83
+LEAN = 72
 MATE = 83
 MATES = 10
 ALL = MATE + MATES
@@ -67,6 +67,14 @@
 SENT = -(-(4 * len(fours()) + 2 * len(twos())) // 8)
 SENT_SIDES = -(-SENT // 8)
 SENT_ALL = SENT + SENT_SIDES
+
+
+def own_plane(tile, front, plane, rows=slice(0, ROWS)):
+    if plane == DISP:
+        return jnp.where(front, tile[LEAN + THICK - 1, rows, :], tile[LEAN, rows, :])
+    if plane >= SCALES:
+        plane += THICK - (plane > DISP)
+    return tile[plane, rows, :]
 
 
 def lanes_of(rows):
@@ -152,43 +160,24 @@
             put(at(f, z), fresh * keep)
 
 
-def fetch_kernel(state, damage, frame, impact, near, far, again, tile, levels, held, struck, arrived):
-    copies = [
-        pltpu.make_async_copy(damage.at[0], levels, arrived.at[10]),
-        pltpu.make_async_copy(frame, held, arrived.at[11]),
-        pltpu.make_async_copy(impact, struck, arrived.at[12]),
-    ]
-    for f in range(10):
-        first = SPARE if f == 9 else at(f, 0)
-        copies.append(
-            pltpu.make_async_copy(state.at[0, f], tile.at[pl.ds(first, THICK)], arrived.at[f])
-        )
-    for copy in copies:
-        copy.start()
-    for copy in (*copies[:3], copies[12]):
-        copy.wait()
+def strip_kernel(tile, near, far, again):
     front = lax.axis_index("ply") == 0
     even = lax.axis_index("hgt") % 2 == 0
-    for z in range(THICK):
-        tile[at(SCALE, z)] = 1.0 - softening * levels[z].astype(jnp.float32)
-    tile[DISP] = jnp.where(front, tile[SPARE + THICK - 1], tile[SPARE])
-    tile[KEEP] = (1 - held[...]).astype(jnp.float32)
-    tile[PUSH] = struck[...].astype(jnp.float32)
     slot = lanes_of(ROWS) // HALO
     for g in range(GROUPS):
-        for copy in copies[3 + 2 * g : min(5 + 2 * g, 12)]:
-            copy.wait()
         first = jnp.zeros((ROWS, LANES), jnp.float32)
         last = first
         for j in range(min(PER_GROUP, OWN - g * PER_GROUP)):
-            plane = tile[g * PER_GROUP + j]
-            first = jnp.where(slot == j, turn(plane, HALO * j), first)
-            last = jnp.where(slot == j, turn(plane, HALO * j + HALO), last)
+            plane = own_plane(tile, front, g * PER_GROUP + j)
+            plane = turn(plane, HALO * j + HALO)
+            first = jnp.where(slot == (j + 1) % PER_GROUP, plane, first)
+            last = jnp.where(slot == j, plane, last)
+        first = turn(first, -HALO)
         near[g] = again[g] = jnp.where(even, last, first)
         far[g] = jnp.where(even, first, last)
 
 
-def side_kernel(state, high, far, low, side, surface):
+def side_kernel(tile, high, far, low, side, surface):
     front = lax.axis_index("ply") == 0
     place = lax.axis_index("hgt")
     even = place % 2 == 0
@@ -206,11 +195,11 @@
     full = []
     for k, pick in enumerate(PICKS):
         if pick is None:
-            main = jnp.where(front, state[0, 9, THICK - 1], state[0, 9, 0])
+            main = own_plane(tile, front, DISP)
             flank = side[DISP]
         else:
             f, less, more = pick[0], pick[1], THICK - 1 - pick[1]
-            main = jnp.where(front, state[0, f, more], state[0, f, less])
+            main = jnp.where(front, tile[at(f, more)], tile[at(f, less)])
             flank = jnp.where(front, side[at(f, more)], side[at(f, less)])
         full.append(jnp.stack([main, flank]))
     up = jnp.where(front, -1.0, 1.0)
@@ -225,14 +214,9 @@
 
 
 def speed_kernel(
-    state, damage, frame, impact, side, mates, fresh, mate, extra, near, far, middle, flank
+    tile, side, mates, fresh, mate, near, far, middle, flank
 ):
     front = lax.axis_index("ply") == 0
-    for z in range(THICK):
-        extra[z] = 1.0 - softening * damage[0, z].astype(jnp.float32)
-    extra[DISP - 72] = jnp.where(front, state[0, 9, THICK - 1], state[0, 9, 0])
-    extra[KEEP - 72] = (1 - frame[...]).astype(jnp.float32)
-    extra[PUSH - 72] = impact[...].astype(jnp.float32)
     core = lax.axis_index("len") % 2
     other = jnp.where(front, 1, 0)
     for k in range(MATES):
@@ -242,10 +226,7 @@
     def look(plane, r, n):
         if plane >= MATE:
             return mate[plane - MATE, :, r : r + n, :]
-        if plane >= 72:
-            main = extra[plane - 72, r : r + n, :]
-        else:
-            main = state[0, plane // THICK, plane % THICK, r : r + n, :]
+        main = own_plane(tile, front, plane, slice(r, r + n))
         return jnp.stack([main, side[plane, r : r + n, :]])
 
     def put(plane, value):
@@ -268,7 +249,7 @@
             out[SENT + g] = pack_sides([flank[way, k] for k in ks])
 
 
-def last_kernel(state, extra, side, fresh, mate, near, far, out, cells):
+def last_kernel(tile, side, fresh, mate, near, far, out, cells):
     front = lax.axis_index("ply") == 0
     index = lax.axis_index("len")
     upper = index % 2 == 0
@@ -276,11 +257,7 @@
     has_bottom = index < lax.axis_size("len") - 1
 
     for plane in range(OWN):
-        if plane >= 72:
-            main = extra[plane - 72]
-        else:
-            main = state[0, plane // THICK, plane % THICK]
-        cells[plane, 0, HALO : HALO + ROWS, :] = main
+        cells[plane, 0, HALO : HALO + ROWS, :] = own_plane(tile, front, plane)
         cells[plane, 1, HALO : HALO + ROWS, :] = side[plane]
     for k in range(MATES):
         cells[MATE + k, :, HALO : HALO + ROWS, :] = mate[k]
@@ -347,7 +324,7 @@
     for z in range(THICK):
         for f, change in enumerate(changes(z, r, n, 2)):
             put(at(SXX + f, z), look(at(SXX + f, z), r, n) + change)
-        out[0, 9, z] = state[0, 9, z] + time_step * look(at(VZ, z), 0, ROWS)[0]
+        out[0, 9, z] = tile[LEAN + z] + time_step * look(at(VZ, z), 0, ROWS)[0]
     new_velocities(look, -2, ROWS + 4, front, writer(-2, ROWS + 4), False)
     for z in range(THICK):
         for f in range(3):
@@ -372,27 +349,21 @@
     )(*args)
 
 
-FETCH_LIMIT = 60 * MIB
-
-
 def per_device(plate_state, damage, frame_mask, impact_mask):
     even = [[2 * i, 2 * i + 1] for i in range(8)]
     odd = [[2 * i + 1, (2 * i + 2) % 16] for i in range(8)]
     strips = shaped(GROUPS, ROWS, LANES)
-    near, far, again = call(
-        fetch_kernel,
-        [strips, strips, strips],
-        (plate_state, damage, frame_mask, impact_mask),
-        limit=FETCH_LIMIT,
-        space=pl.ANY,
-        scratch=[
-            pltpu.VMEM((OWN + THICK, ROWS, LANES), jnp.float32),
-            pltpu.VMEM((THICK, ROWS, LANES), jnp.int32),
-            pltpu.VMEM((ROWS, LANES), jnp.int32),
-            pltpu.VMEM((ROWS, LANES), jnp.int32),
-            pltpu.SemaphoreType.DMA((13,)),
-        ],
-    )
+    tile = jnp.zeros((90, ROWS, LANES), jnp.float32)
+    tile = lax.dynamic_update_slice(tile, plate_state.reshape(80, ROWS, LANES), (0, 0, 0))
+    tile, damage, frame_mask, impact_mask = lax.optimization_barrier(
+        (tile, damage, frame_mask, impact_mask)
+    )
+    whole = jnp.concatenate([damage[0], frame_mask[None], impact_mask[None]])
+    which = lax.broadcasted_iota(jnp.int32, whole.shape, 0)
+    slope = jnp.where(which < THICK, -softening, jnp.where(which == THICK, -1.0, 1.0))
+    extra = jnp.where(which > THICK, 0.0, 1.0) + slope * whole.astype(jnp.float32)
+    tile = lax.dynamic_update_slice(tile, extra, (80, 0, 0))
+    near, far, again = call(strip_kernel, [strips, strips, strips], (tile,))
     swap = [(i, j) for pair in odd[:-1] for i, j in (pair, pair[::-1])]
     both = lambda pairs: [(i, j) for pair in pairs for i, j in (pair, pair[::-1])]
     high = lax.ppermute(near, "hgt", both(even[4:]))
@@ -401,20 +372,19 @@
     side, surface = call(
         side_kernel,
         [shaped(OWN, ROWS, LANES), shaped(MATE_SENT, ROWS, LANES)],
-        (plate_state, high, far, low),
+        (tile, high, far, low),
     )
     mates = lax.all_gather(surface, "ply")
     sent = shaped(SENT_ALL, HALO, LANES)
-    fresh, mate, extra, near, far = call(
+    fresh, mate, near, far = call(
         speed_kernel,
         [
             shaped(27, 2, ROWS, LANES),
             shaped(MATES, 2, ROWS, LANES),
-            shaped(11, ROWS, LANES),
             sent,
             sent,
         ],
-        (plate_state, damage, frame_mask, impact_mask, side, mates),
+        (tile, side, mates),
         scratch=[pltpu.VMEM((2, SENT, HALO, LANES), jnp.float32)] * 2,
     )
     far = lax.ppermute(far, "len", swap)
@@ -422,7 +392,7 @@
     return call(
         last_kernel,
         shaped(1, 10, THICK, ROWS, LANES),
-        (plate_state, extra, side, fresh, mate, near, far),
+        (tile, side, fresh, mate, near, far),
         scratch=[pltpu.VMEM((ALL, 2, ROWS + 2 * HALO, LANES), jnp.float32)],
     )
 

time: 36.2 us -> 35.7 us (0.986)
  Pallas kernels: 7.3 us -> 5.09 us
  local copies, waits for them, and re-layouts: 0.01 us -> 1.85 us
    pallas_call x4, Pallas kernels: 7.3 us -> 5.09 us  [call(): pl.pallas_call(kernel, out_shape=outs, in_specs=[pl.BlockSpec(memory_spac...]
    dynamic_update_slice x0 -> x1, local copies, waits for them, and re-layouts: none -> 1.17 us  [per_device(): lax.dynamic_update_slice(tile, plate_state.reshape(80, ROWS, LANES), (0,...]
    unnamed x8 -> x6, local copies, waits for them, and re-layouts: 0.01 us -> 0.68 us
where the time goes in v6:
time: 35.7 us; the launch traced here: 35.4 us
  starting transfers between devices  19.9 us (56%)
  blocking collectives  6.24 us (17%)
  Pallas kernels  5.09 us (14%)
  waiting for transfers between devices  2.11 us (6%)
  local copies, waits for them, and re-layouts  1.85 us (5%)
    ppermute x1, starting transfers between devices, per_device(): far = lax.ppermute(far, 'hgt', swap)  8.17 us
    ppermute x1, starting transfers between devices, per_device(): far = lax.ppermute(far, 'len', swap)  7.1 us
    pallas_call x4, Pallas kernels, call(): pl.pallas_call(kernel, out_shape=outs, in_specs=[pl.BlockSpec(memory_spac...  5.09 us
    all_gather x1, blocking collectives, per_device(): mates = lax.all_gather(surface, 'ply')  4.14 us
    ppermute x1, starting transfers between devices, per_device(): high = lax.ppermute(near, 'hgt', both(even[4:]))  3.99 us
    all_gather x1, blocking collectives, per_device(): near = lax.all_gather(near, 'len', axis_index_groups=even)  2.1 us
    ppermute x1, waiting for transfers between devices, per_device(): far = lax.ppermute(far, 'len', swap)  1.33 us
    dynamic_update_slice x1, local copies, waits for them, and re-layouts, per_device(): lax.dynamic_update_slice(tile, plate_state.reshape(80, ROWS, LANES), (0,...  1.17 us
  transfers between devices with their start and end apart: 4, of which 2 were waited for; matrix products, arithmetic and copies ran while one was open for 0% of the time, Pallas kernels for 0%

profile of v6, /device:TPU:31, one launch (start us, length us, event | category | flops | bytes accessed | tf_op | source)
XLA Modules:
  0.0 35.4 jit_solution(17561171690693543689)
XLA Ops:
  0.0 0.0 copy-start
  0.0 0.0 copy-start.2
  0.0 1.2 %dynamic_update_slice.6 = f32[90,16,128]{2,1,0:T(8,128)S(1)} pad(f32[80,16,128]{2,1,0:T(8,128)} %bitcast.8, f32[]{:T(128)} %constant.7.clone.1), padding=0_10x0_0x0_0 | pad | bytes 1392644 | tf_op jit(solution)/shard_map/dynamic_update_slice | solution.py:357
  1.2 0.0 copy-start.1
  1.2 0.0 copy-done
  1.2 0.0 copy-done.2
  1.2 0.7 %copy-done.1 = s32[16,128]{1,0:T(8,128)S(1)} copy-done((s32[16,128]{1,0:T(8,128)S(1)}, s32[16,128]{1,0:T(8,128)}, u32[]{:S(2)}) %copy-start.1) | copy-done | bytes 8216
  1.9 0.1 fusion.2.tile
  2.0 0.4 %shard_map.46 = (f32[6,16,128]{2,1,0:T(8,128)S(1)}, f32[6,16,128]{2,1,0:T(8,128)S(1)}, f32[6,16,128]{2,1,0:T(8,128)S(1)}) custom-call(f32[90,16,128]{2,1,0:T(8,128)S(1)} %fusion.2.tile), custom_call_target="tpu_custom_call" | custom-call | tf_op jit(solution)/shard_map/pallas_call | solution.py:342
  2.4 4.0 %collective-permute-start = (f32[6,16,128]{2,1,0:T(8,128)S(1)}, f32[6,16,128]{2,1,0:T(8,128)S(1)}, u32[]{:S(2)}, u32[]{:S(2)}) collective-permute-start(f32[6,16,128]{2,1,0:T(8,128)S(1)} %get-tuple-element.22), channel_id=1, source_target_pairs={{8,9},{9,8},{10,11},{11,10},{12,13},{13,12},{14,15},{15,14},{24,25... | collective-permute-start | bytes 147464 | tf_op jit(solution)/shard_map/ppermute | solution.py:369
  6.4 8.2 %collective-permute-start.1 = (f32[6,16,128]{2,1,0:T(8,128)S(1)}, f32[6,16,128]{2,1,0:T(8,128)S(1)}, u32[]{:S(2)}, u32[]{:S(2)}) collective-permute-start(f32[6,16,128]{2,1,0:T(8,128)S(1)} %get-tuple-element.23), channel_id=1, source_target_pairs={{1,2},{2,1},{3,4},{4,3},{5,6},{6,5},{7,8},{8,7},{9,10},{10,9},{11,... | collective-permute-start | bytes 147464 | tf_op jit(solution)/shard_map/ppermute | solution.py:370
  14.6 0.7 %collective-permute-start.2 = (f32[6,16,128]{2,1,0:T(8,128)S(1)}, f32[6,16,128]{2,1,0:T(8,128)S(1)}, u32[]{:S(2)}, u32[]{:S(2)}) collective-permute-start(f32[6,16,128]{2,1,0:T(8,128)S(1)} %get-tuple-element.24), channel_id=1, source_target_pairs={{0,1},{1,0},{2,3},{3,2},{4,5},{5,4},{6,7},{7,6},{16,17},{17,16},{1... | collective-permute-start | bytes 147464 | tf_op jit(solution)/shard_map/ppermute | solution.py:371
  15.3 0.0 collective-permute-done.high
  15.3 0.8 %collective-permute-done.1.far = f32[6,16,128]{2,1,0:T(8,128)S(1)} collective-permute-done((f32[6,16,128]{2,1,0:T(8,128)S(1)}, f32[6,16,128]{2,1,0:T(8,128)S(1)}, u32[]{:S(2)}, u32[]{:S(2)}) %collective-permute-start.1) | collective-permute-done | bytes 49184 | tf_op jit(solution)/shard_map/ppermute | solution.py:370
  16.1 0.0 collective-permute-done.2.low
  16.1 0.5 %shard_map.47 = (f32[83,16,128]{2,1,0:T(8,128)S(1)}, f32[12,16,128]{2,1,0:T(8,128)S(1)}) custom-call(f32[90,16,128]{2,1,0:T(8,128)S(1)} %fusion.2.tile, f32[6,16,128]{2,1,0:T(8,128)S(1)} %collective-permute-done.high, f32[6,16,128]{2,1,0:T(8,128)S(1)} %collective-permute-done.1.far, f32[6,16,128]{2,1,0:T(8,128)S(1)} %collective-permute-done.2.low), custom_call_target="tpu_custom_call" | custom-call | tf_op jit(solution)/shard_map/pallas_call | solution.py:342
  16.6 4.1 %all-gather = f32[24,16,128]{2,1,0:T(8,128)S(1)} all-gather(f32[12,16,128]{2,1,0:T(8,128)S(1)} %get-tuple-element.26), channel_id=2, replica_groups=mesh['ply'=2,'len'=16,'hgt'=16] {'ply'}, dimensions={0}, use_global_device_ids=true | all-gather | bytes 294912 | tf_op jit(solution)/shard_map/all_gather | solution.py:377
  20.7 0.8 %shard_map.48 = (f32[27,2,16,128]{3,2,1,0:T(8,128)S(1)}, f32[10,2,16,128]{3,2,1,0:T(8,128)S(1)}, f32[50,8,128]{2,1,0:T(8,128)S(1)}, f32[50,8,128]{2,1,0:T(8,128)S(1)}) custom-call(f32[90,16,128]{2,1,0:T(8,128)S(1)} %fusion.2.tile, f32[83,16,128]{2,1,0:T(8,128)S(1)} %get-tuple-element.25.side, f32[2,12,16,128]{3,2,1,0:T(8,128)S(1)} %bitcast.7), custom_call_target="tpu_custom_call" | custom-call | tf_op jit(solution)/shard_map/pallas_call | solution.py:342
  21.5 7.1 %collective-permute-start.3 = (f32[50,8,128]{2,1,0:T(8,128)S(1)}, f32[50,8,128]{2,1,0:T(8,128)S(1)}, u32[]{:S(2)}, u32[]{:S(2)}) collective-permute-start(f32[50,8,128]{2,1,0:T(8,128)S(1)} %get-tuple-element.30), channel_id=1, source_target_pairs={{16,32},{32,16},{48,64},{64,48},{80,96},{96,80},{112,128},{128,112... | collective-permute-start | bytes 614408 | tf_op jit(solution)/shard_map/ppermute | solution.py:390
  28.6 2.1 %all-gather.1 = f32[100,8,128]{2,1,0:T(8,128)S(1)} all-gather(f32[50,8,128]{2,1,0:T(8,128)S(1)} %get-tuple-element.29), channel_id=3, replica_groups={{0,16},{32,48},{64,80},{96,112},{128,144},{160,176},{192,208},{224,240}..., dimensions={0}, use_global_device_ids=true | all-gather | bytes 614400 | tf_op jit(solution)/shard_map/all_gather | solution.py:391
  30.7 1.3 %collective-permute-done.3.far = f32[50,8,128]{2,1,0:T(8,128)S(1)} collective-permute-done((f32[50,8,128]{2,1,0:T(8,128)S(1)}, f32[50,8,128]{2,1,0:T(8,128)S(1)}, u32[]{:S(2)}, u32[]{:S(2)}) %collective-permute-start.3) | collective-permute-done | bytes 204832 | tf_op jit(solution)/shard_map/ppermute | solution.py:390
  32.1 3.3 %shard_map.49 = f32[1,10,8,16,128]{4,3,2,1,0:T(8,128)} custom-call(f32[90,16,128]{2,1,0:T(8,128)S(1)} %fusion.2.tile, f32[83,16,128]{2,1,0:T(8,128)S(1)} %get-tuple-element.25.side, f32[27,2,16,128]{3,2,1,0:T(8,128)S(1)} %get-tuple-element.27.fresh, f32[10,2,16,128]{3,2,1,0:T(8,128)S(1)} %get-tuple-element.28.mate, f32[2,50,8,128]{3,2,1,0:T(8,128)S(1)} %bitcast.6, ...), custom_call_target="tpu_custom_call" | custom-call | tf_op jit(solution)/shard_map/pallas_call | solution.py:342
  (2 shorter events, 0.0 us)
Async XLA Ops:
  0.0 1.2 %copy-start = (s32[1,8,16,128]{3,2,1,0:T(8,128)S(1)}, s32[1,8,16,128]{3,2,1,0:T(8,128)}, u32[]{:S(2)}) copy-start(s32[1,8,16,128]{3,2,1,0:T(8,128)} %param.5) | copy-start | bytes 196612
  0.0 1.2 %copy-start.2 = (s32[16,128]{1,0:T(8,128)S(1)}, s32[16,128]{1,0:T(8,128)}, u32[]{:S(2)}) copy-start(s32[16,128]{1,0:T(8,128)} %param.6) | copy-start | bytes 24580
  1.2 0.7 %copy-start.1 = (s32[16,128]{1,0:T(8,128)S(1)}, s32[16,128]{1,0:T(8,128)}, u32[]{:S(2)}) copy-start(s32[16,128]{1,0:T(8,128)} %param.7) | copy-start | bytes 24580
  2.4 12.9 %collective-permute-start = (f32[6,16,128]{2,1,0:T(8,128)S(1)}, f32[6,16,128]{2,1,0:T(8,128)S(1)}, u32[]{:S(2)}, u32[]{:S(2)}) collective-permute-start(f32[6,16,128]{2,1,0:T(8,128)S(1)} %get-tuple-element.22), channel_id=1, source_target_pairs={{8,9},{9,8},{10,11},{11,10},{12,13},{13,12},{14,15},{15,14},{24,25... | collective-permute-start | bytes 147464 | tf_op jit(solution)/shard_map/ppermute | solution.py:369
  6.4 9.6 %collective-permute-start.1 = (f32[6,16,128]{2,1,0:T(8,128)S(1)}, f32[6,16,128]{2,1,0:T(8,128)S(1)}, u32[]{:S(2)}, u32[]{:S(2)}) collective-permute-start(f32[6,16,128]{2,1,0:T(8,128)S(1)} %get-tuple-element.23), channel_id=1, source_target_pairs={{1,2},{2,1},{3,4},{4,3},{5,6},{6,5},{7,8},{8,7},{9,10},{10,9},{11,... | collective-permute-start | bytes 147464 | tf_op jit(solution)/shard_map/ppermute | solution.py:370
  14.6 1.5 %collective-permute-start.2 = (f32[6,16,128]{2,1,0:T(8,128)S(1)}, f32[6,16,128]{2,1,0:T(8,128)S(1)}, u32[]{:S(2)}, u32[]{:S(2)}) collective-permute-start(f32[6,16,128]{2,1,0:T(8,128)S(1)} %get-tuple-element.24), channel_id=1, source_target_pairs={{0,1},{1,0},{2,3},{3,2},{4,5},{5,4},{6,7},{7,6},{16,17},{17,16},{1... | collective-permute-start | bytes 147464 | tf_op jit(solution)/shard_map/ppermute | solution.py:371
  21.5 10.5 %collective-permute-start.3 = (f32[50,8,128]{2,1,0:T(8,128)S(1)}, f32[50,8,128]{2,1,0:T(8,128)S(1)}, u32[]{:S(2)}, u32[]{:S(2)}) collective-permute-start(f32[50,8,128]{2,1,0:T(8,128)S(1)} %get-tuple-element.30), channel_id=1, source_target_pairs={{16,32},{32,16},{48,64},{64,48},{80,96},{96,80},{112,128},{128,112... | collective-permute-start | bytes 614408 | tf_op jit(solution)/shard_map/ppermute | solution.py:390

commit v7 on v6

--- a/solution.py
+++ b/solution.py
@@ -72,9 +72,12 @@
 def own_plane(tile, front, plane, rows=slice(0, ROWS)):
     if plane == DISP:
         return jnp.where(front, tile[LEAN + THICK - 1, rows, :], tile[LEAN, rows, :])
-    if plane >= SCALES:
-        plane += THICK - (plane > DISP)
-    return tile[plane, rows, :]
+    if plane < SCALES:
+        return tile[plane, rows, :]
+    given = tile[plane + THICK - (plane > DISP), rows, :]
+    if plane < DISP:
+        return 1.0 - softening * given
+    return 1.0 - given if plane == KEEP else given
 
 
 def lanes_of(rows):
@@ -359,9 +362,7 @@
         (tile, damage, frame_mask, impact_mask)
     )
     whole = jnp.concatenate([damage[0], frame_mask[None], impact_mask[None]])
-    which = lax.broadcasted_iota(jnp.int32, whole.shape, 0)
-    slope = jnp.where(which < THICK, -softening, jnp.where(which == THICK, -1.0, 1.0))
-    extra = jnp.where(which > THICK, 0.0, 1.0) + slope * whole.astype(jnp.float32)
+    extra = whole.astype(jnp.float32)
     tile = lax.dynamic_update_slice(tile, extra, (80, 0, 0))
     near, far, again = call(strip_kernel, [strips, strips, strips], (tile,))
     swap = [(i, j) for pair in odd[:-1] for i, j in (pair, pair[::-1])]

time: 35.7 us -> 34.8 us (0.975)
  local copies, waits for them, and re-layouts: 1.85 us -> 1.18 us
    unnamed x6, local copies, waits for them, and re-layouts: 0.68 us -> 0.01 us
where the time goes in v7:
time: 34.8 us; the launch traced here: 34.6 us
  starting transfers between devices  19.9 us (57%)
  blocking collectives  6.24 us (18%)
  Pallas kernels  5.08 us (15%)
  waiting for transfers between devices  2.11 us (6%)
  local copies, waits for them, and re-layouts  1.18 us (3%)
    ppermute x1, starting transfers between devices, per_device(): far = lax.ppermute(far, 'hgt', swap)  8.17 us
    ppermute x1, starting transfers between devices, per_device(): far = lax.ppermute(far, 'len', swap)  7.1 us
    pallas_call x4, Pallas kernels, call(): pl.pallas_call(kernel, out_shape=outs, in_specs=[pl.BlockSpec(memory_spac...  5.08 us
    all_gather x1, blocking collectives, per_device(): mates = lax.all_gather(surface, 'ply')  4.14 us
    ppermute x1, starting transfers between devices, per_device(): high = lax.ppermute(near, 'hgt', both(even[4:]))  3.99 us
    all_gather x1, blocking collectives, per_device(): near = lax.all_gather(near, 'len', axis_index_groups=even)  2.1 us
    ppermute x1, waiting for transfers between devices, per_device(): far = lax.ppermute(far, 'len', swap)  1.33 us
    dynamic_update_slice x1, local copies, waits for them, and re-layouts, per_device(): lax.dynamic_update_slice(tile, plate_state.reshape(80, ROWS, LANES), (0,...  1.17 us
  transfers between devices with their start and end apart: 4, of which 2 were waited for; matrix products, arithmetic and copies ran while one was open for 0% of the time, Pallas kernels for 0%

profile of v7, /device:TPU:31, one launch (start us, length us, event | category | flops | bytes accessed | tf_op | source)
XLA Modules:
  0.0 34.6 jit_solution(15345838814910518596)
XLA Ops:
  0.0 0.0 copy-start
  0.0 0.0 copy-start.1
  0.0 0.0 copy-start.2
  0.0 1.2 %dynamic_update_slice.6 = f32[90,16,128]{2,1,0:T(8,128)S(1)} pad(f32[80,16,128]{2,1,0:T(8,128)} %bitcast.8, f32[]{:T(128)} %constant.0.clone.1), padding=0_10x0_0x0_0 | pad | bytes 1392644 | tf_op jit(solution)/shard_map/dynamic_update_slice | solution.py:360
  1.2 0.0 copy-done
  1.2 0.0 copy-done.1
  1.2 0.0 copy-done.2
  1.2 0.4 %shard_map.46 = (f32[6,16,128]{2,1,0:T(8,128)S(1)}, f32[6,16,128]{2,1,0:T(8,128)S(1)}, f32[6,16,128]{2,1,0:T(8,128)S(1)}) custom-call(f32[90,16,128]{2,1,0:T(8,128)S(1)} %fusion.tile), custom_call_target="tpu_custom_call" | custom-call | tf_op jit(solution)/shard_map/pallas_call | solution.py:345
  1.7 4.0 %collective-permute-start = (f32[6,16,128]{2,1,0:T(8,128)S(1)}, f32[6,16,128]{2,1,0:T(8,128)S(1)}, u32[]{:S(2)}, u32[]{:S(2)}) collective-permute-start(f32[6,16,128]{2,1,0:T(8,128)S(1)} %get-tuple-element.22), channel_id=1, source_target_pairs={{8,9},{9,8},{10,11},{11,10},{12,13},{13,12},{14,15},{15,14},{24,25... | collective-permute-start | bytes 147464 | tf_op jit(solution)/shard_map/ppermute | solution.py:370
  5.7 8.2 %collective-permute-start.1 = (f32[6,16,128]{2,1,0:T(8,128)S(1)}, f32[6,16,128]{2,1,0:T(8,128)S(1)}, u32[]{:S(2)}, u32[]{:S(2)}) collective-permute-start(f32[6,16,128]{2,1,0:T(8,128)S(1)} %get-tuple-element.23), channel_id=1, source_target_pairs={{1,2},{2,1},{3,4},{4,3},{5,6},{6,5},{7,8},{8,7},{9,10},{10,9},{11,... | collective-permute-start | bytes 147464 | tf_op jit(solution)/shard_map/ppermute | solution.py:371
  13.8 0.7 %collective-permute-start.2 = (f32[6,16,128]{2,1,0:T(8,128)S(1)}, f32[6,16,128]{2,1,0:T(8,128)S(1)}, u32[]{:S(2)}, u32[]{:S(2)}) collective-permute-start(f32[6,16,128]{2,1,0:T(8,128)S(1)} %get-tuple-element.24), channel_id=1, source_target_pairs={{0,1},{1,0},{2,3},{3,2},{4,5},{5,4},{6,7},{7,6},{16,17},{17,16},{1... | collective-permute-start | bytes 147464 | tf_op jit(solution)/shard_map/ppermute | solution.py:372
  14.5 0.0 collective-permute-done.high
  14.5 0.8 %collective-permute-done.1.far = f32[6,16,128]{2,1,0:T(8,128)S(1)} collective-permute-done((f32[6,16,128]{2,1,0:T(8,128)S(1)}, f32[6,16,128]{2,1,0:T(8,128)S(1)}, u32[]{:S(2)}, u32[]{:S(2)}) %collective-permute-start.1) | collective-permute-done | bytes 49184 | tf_op jit(solution)/shard_map/ppermute | solution.py:371
  15.3 0.0 collective-permute-done.2.low
  15.3 0.5 %shard_map.47 = (f32[83,16,128]{2,1,0:T(8,128)S(1)}, f32[12,16,128]{2,1,0:T(8,128)S(1)}) custom-call(f32[90,16,128]{2,1,0:T(8,128)S(1)} %fusion.tile, f32[6,16,128]{2,1,0:T(8,128)S(1)} %collective-permute-done.high, f32[6,16,128]{2,1,0:T(8,128)S(1)} %collective-permute-done.1.far, f32[6,16,128]{2,1,0:T(8,128)S(1)} %collective-permute-done.2.low), custom_call_target="tpu_custom_call" | custom-call | tf_op jit(solution)/shard_map/pallas_call | solution.py:345
  15.8 4.1 %all-gather = f32[24,16,128]{2,1,0:T(8,128)S(1)} all-gather(f32[12,16,128]{2,1,0:T(8,128)S(1)} %get-tuple-element.26), channel_id=2, replica_groups=mesh['ply'=2,'len'=16,'hgt'=16] {'ply'}, dimensions={0}, use_global_device_ids=true | all-gather | bytes 294912 | tf_op jit(solution)/shard_map/all_gather | solution.py:378
  20.0 0.8 %shard_map.48 = (f32[27,2,16,128]{3,2,1,0:T(8,128)S(1)}, f32[10,2,16,128]{3,2,1,0:T(8,128)S(1)}, f32[50,8,128]{2,1,0:T(8,128)S(1)}, f32[50,8,128]{2,1,0:T(8,128)S(1)}) custom-call(f32[90,16,128]{2,1,0:T(8,128)S(1)} %fusion.tile, f32[83,16,128]{2,1,0:T(8,128)S(1)} %get-tuple-element.25.side, f32[2,12,16,128]{3,2,1,0:T(8,128)S(1)} %bitcast.7), custom_call_target="tpu_custom_call" | custom-call | tf_op jit(solution)/shard_map/pallas_call | solution.py:345
  20.8 7.1 %collective-permute-start.3 = (f32[50,8,128]{2,1,0:T(8,128)S(1)}, f32[50,8,128]{2,1,0:T(8,128)S(1)}, u32[]{:S(2)}, u32[]{:S(2)}) collective-permute-start(f32[50,8,128]{2,1,0:T(8,128)S(1)} %get-tuple-element.30), channel_id=1, source_target_pairs={{16,32},{32,16},{48,64},{64,48},{80,96},{96,80},{112,128},{128,112... | collective-permute-start | bytes 614408 | tf_op jit(solution)/shard_map/ppermute | solution.py:391
  27.9 2.1 %all-gather.1 = f32[100,8,128]{2,1,0:T(8,128)S(1)} all-gather(f32[50,8,128]{2,1,0:T(8,128)S(1)} %get-tuple-element.29), channel_id=3, replica_groups={{0,16},{32,48},{64,80},{96,112},{128,144},{160,176},{192,208},{224,240}..., dimensions={0}, use_global_device_ids=true | all-gather | bytes 614400 | tf_op jit(solution)/shard_map/all_gather | solution.py:392
  30.0 1.3 %collective-permute-done.3.far = f32[50,8,128]{2,1,0:T(8,128)S(1)} collective-permute-done((f32[50,8,128]{2,1,0:T(8,128)S(1)}, f32[50,8,128]{2,1,0:T(8,128)S(1)}, u32[]{:S(2)}, u32[]{:S(2)}) %collective-permute-start.3) | collective-permute-done | bytes 204832 | tf_op jit(solution)/shard_map/ppermute | solution.py:391
  31.3 3.4 %shard_map.49 = f32[1,10,8,16,128]{4,3,2,1,0:T(8,128)} custom-call(f32[90,16,128]{2,1,0:T(8,128)S(1)} %fusion.tile, f32[83,16,128]{2,1,0:T(8,128)S(1)} %get-tuple-element.25.side, f32[27,2,16,128]{3,2,1,0:T(8,128)S(1)} %get-tuple-element.27.fresh, f32[10,2,16,128]{3,2,1,0:T(8,128)S(1)} %get-tuple-element.28.mate, f32[2,50,8,128]{3,2,1,0:T(8,128)S(1)} %bitcast.6, ...), custom_call_target="tpu_custom_call" | custom-call | tf_op jit(solution)/shard_map/pallas_call | solution.py:345
  (1 shorter events, 0.0 us)
Async XLA Ops:
  0.0 1.2 %copy-start = (s32[1,8,16,128]{3,2,1,0:T(8,128)S(1)}, s32[1,8,16,128]{3,2,1,0:T(8,128)}, u32[]{:S(2)}) copy-start(s32[1,8,16,128]{3,2,1,0:T(8,128)} %param.5) | copy-start | bytes 196612
  0.0 1.2 %copy-start.1 = (s32[16,128]{1,0:T(8,128)S(1)}, s32[16,128]{1,0:T(8,128)}, u32[]{:S(2)}) copy-start(s32[16,128]{1,0:T(8,128)} %param.7) | copy-start | bytes 24580
  0.0 1.2 %copy-start.2 = (s32[16,128]{1,0:T(8,128)S(1)}, s32[16,128]{1,0:T(8,128)}, u32[]{:S(2)}) copy-start(s32[16,128]{1,0:T(8,128)} %param.6) | copy-start | bytes 24580
  1.7 12.9 %collective-permute-start = (f32[6,16,128]{2,1,0:T(8,128)S(1)}, f32[6,16,128]{2,1,0:T(8,128)S(1)}, u32[]{:S(2)}, u32[]{:S(2)}) collective-permute-start(f32[6,16,128]{2,1,0:T(8,128)S(1)} %get-tuple-element.22), channel_id=1, source_target_pairs={{8,9},{9,8},{10,11},{11,10},{12,13},{13,12},{14,15},{15,14},{24,25... | collective-permute-start | bytes 147464 | tf_op jit(solution)/shard_map/ppermute | solution.py:370
  5.7 9.6 %collective-permute-start.1 = (f32[6,16,128]{2,1,0:T(8,128)S(1)}, f32[6,16,128]{2,1,0:T(8,128)S(1)}, u32[]{:S(2)}, u32[]{:S(2)}) collective-permute-start(f32[6,16,128]{2,1,0:T(8,128)S(1)} %get-tuple-element.23), channel_id=1, source_target_pairs={{1,2},{2,1},{3,4},{4,3},{5,6},{6,5},{7,8},{8,7},{9,10},{10,9},{11,... | collective-permute-start | bytes 147464 | tf_op jit(solution)/shard_map/ppermute | solution.py:371
  13.8 1.5 %collective-permute-start.2 = (f32[6,16,128]{2,1,0:T(8,128)S(1)}, f32[6,16,128]{2,1,0:T(8,128)S(1)}, u32[]{:S(2)}, u32[]{:S(2)}) collective-permute-start(f32[6,16,128]{2,1,0:T(8,128)S(1)} %get-tuple-element.24), channel_id=1, source_target_pairs={{0,1},{1,0},{2,3},{3,2},{4,5},{5,4},{6,7},{7,6},{16,17},{17,16},{1... | collective-permute-start | bytes 147464 | tf_op jit(solution)/shard_map/ppermute | solution.py:372
  20.8 10.5 %collective-permute-start.3 = (f32[50,8,128]{2,1,0:T(8,128)S(1)}, f32[50,8,128]{2,1,0:T(8,128)S(1)}, u32[]{:S(2)}, u32[]{:S(2)}) collective-permute-start(f32[50,8,128]{2,1,0:T(8,128)S(1)} %get-tuple-element.30), channel_id=1, source_target_pairs={{16,32},{32,16},{48,64},{64,48},{80,96},{96,80},{112,128},{128,112... | collective-permute-start | bytes 614408 | tf_op jit(solution)/shard_map/ppermute | solution.py:391
